TPU v7x, 32 devices: a whole 2x2x4 slice. The times are simulated.
32 devices in a mesh: dp: 16 (over z, y, x), fsdp: 2 (over core).
Axes of the slice: x: 2, y: 2, z: 4, core: 2. Of those that a mesh axis runs over, the one named last changes fastest.
Arguments:
- teacher_feat: bfloat16 [1024, 256], P(('dp', 'fsdp')), may hold values from -1 to 1
- student_feat: bfloat16 [1024, 256], P(('dp', 'fsdp')), may hold values from -1 to 1
- crop_weight: bfloat16 [1024], P(('dp', 'fsdp')), may hold values from -96 to 96
- teacher_v: bfloat16 [256, 32768], P(None, 'fsdp'), may hold values from -2 to 2
- student_v: bfloat16 [256, 32768], P(None, 'fsdp'), may hold values from -2 to 2
Outputs:
- grad_v: float32 [256, 32768], P('dp', 'fsdp')
- grad_feat: float32 [1024, 256], P(('dp', 'fsdp'))
All inputs are finite; a program needn't handle non-finite values.
Results may differ from a plain program's by a relative error of at most 0.0073.
Values may be sent and summed in bfloat16 or wider, within the bound.
No kernel may reach another device: no remote copies, remote signals or barrier semaphores. Data moves between devices by JAX's collectives and lax.ppermute only.
A program may use at most 128 MiB of HBM per device.

v0:
```python
import functools
import math

import jax
import jax.numpy as jnp
from jax import lax
from jax.experimental import pallas as pl
from jax.experimental.pallas import tpu as pltpu
from jax.sharding import PartitionSpec as P

ITERS = 3

teacher_temp = 0.04
student_temp = 0.1
epsilon = 1e-06

TILE = 256
LANES = 128
VMEM_BYTES = 24 << 20
KEPT_BYTES = 16 << 20

EVERY = ("dp", "fsdp")


def unit_rows(values):
    floats = values.astype(jnp.float32)
    length = jnp.sqrt(jnp.sum(floats * floats, axis=1, keepdims=True) + epsilon)
    return (floats / length, length)


def unit_columns(values):
    floats = values.astype(jnp.float32)
    length = jnp.sqrt(jnp.sum(floats * floats, axis=0, keepdims=True) + epsilon)
    return (floats / length, length)


COPY_BYTES = 1 << 22


def share(values, axes):
    count = lax.axis_size(axes)
    if count * values.size * values.dtype.itemsize > COPY_BYTES:
        return lax.all_gather(values, axes)
    return lax.all_to_all(jnp.broadcast_to(values, (count, *values.shape)), axes, 0, 0)


def add_up(values):
    if lax.axis_size(EVERY) * values.size * values.dtype.itemsize > COPY_BYTES:
        return lax.psum(values, EVERY)
    return jnp.sum(share(values, EVERY), axis=0)


def plain_body(teacher_feat, student_feat, crop_weight, teacher_v, student_v):
    fsdp = lax.axis_size("fsdp")
    devices = lax.axis_size("dp") * fsdp
    own_rows, width = teacher_feat.shape
    crops = own_rows * devices
    block = teacher_v.shape[1] // lax.axis_size("dp")
    prototypes = block * devices
    first = lax.axis_index("dp") * block

    teacher_hat, _ = unit_rows(teacher_feat)
    student_hat, student_len = unit_rows(student_feat)
    units = jnp.concatenate(
        [teacher_hat.astype(jnp.bfloat16), student_hat.astype(jnp.bfloat16)], axis=1
    )
    units = share(share(units, "dp"), "fsdp").reshape(crops, 2 * width)
    teacher_unit, student_unit = units[:, :width], units[:, width:]

    teacher_w, _ = unit_columns(lax.dynamic_slice_in_dim(teacher_v, first, block, 1))
    student_w, student_wlen = unit_columns(lax.dynamic_slice_in_dim(student_v, first, block, 1))
    student_wunit = student_w.astype(jnp.bfloat16)

    mass = jnp.exp(
        jnp.dot(teacher_unit, teacher_w.astype(jnp.bfloat16), preferred_element_type=jnp.float32)
        / teacher_temp
    )
    student_mass = jnp.exp(
        jnp.dot(student_unit, student_wunit, preferred_element_type=jnp.float32) / student_temp
    )
    student_part = jnp.sum(student_mass, axis=1)

    crop_scale = None
    for sweep in range(ITERS):
        scaled = mass if sweep == 0 else mass * crop_scale[:, None]
        proto_scale = 1.0 / (prototypes * jnp.sum(scaled, axis=0))
        crop_part = jnp.sum(mass * proto_scale[None, :], axis=1)
        if sweep == 0:
            placed = jnp.zeros((fsdp, crops // (fsdp * own_rows), own_rows), jnp.float32)
            own = crop_weight.astype(jnp.float32)[None, None]
            spot = (lax.axis_index("fsdp"), lax.axis_index("dp"), 0)
            placed = lax.dynamic_update_slice(placed, own, spot).reshape(crops)
            sums = add_up(jnp.stack([crop_part, student_part, placed]))
            crop_mass, student_total, weights = sums[0], sums[1], sums[2]
        else:
            crop_mass = add_up(crop_part)
        crop_scale = 1.0 / (crops * crop_mass)

    target = crops * (mass * crop_scale[:, None] * proto_scale[None, :])
    student_prob = student_mass / student_total[:, None]
    gradient = ((student_prob - target) * weights[:, None] / student_temp).astype(jnp.bfloat16)
    feature_part = lax.dot_general(
        gradient, student_wunit, (((1,), (1,)), ((), ())), preferred_element_type=jnp.float32
    )
    weight_grad = lax.dot_general(
        student_unit, gradient, (((0,), (0,)), ((), ())), preferred_element_type=jnp.float32
    )
    weight_dot = jnp.sum(student_w * weight_grad, axis=0, keepdims=True)
    grad_block = (weight_grad - student_w * weight_dot) / student_wlen

    feature_sent = feature_part.astype(jnp.bfloat16).reshape(fsdp, -1, own_rows, width)
    feature_sent = jnp.swapaxes(feature_sent, 0, 1).reshape(devices, own_rows, width)
    feature_all = lax.all_to_all(feature_sent, EVERY, 0, 0)
    feature_grad = jnp.sum(feature_all.astype(jnp.float32), axis=0)
    grad_feat = (
        feature_grad - student_hat * jnp.sum(student_hat * feature_grad, axis=1, keepdims=True)
    ) / student_len
    grad_v = lax.all_to_all(grad_block.astype(jnp.bfloat16), "dp", 0, 1, tiled=True)
    return (grad_v.astype(jnp.float32), grad_feat)


def call(kernel, out_shape, flops=0, moved=0, exps=0, **more):
    return pl.pallas_call(
        kernel,
        out_shape=out_shape,
        compiler_params=pltpu.CompilerParams(vmem_limit_bytes=VMEM_BYTES),
        cost_estimate=pl.CostEstimate(flops=flops, bytes_accessed=moved, transcendentals=exps),
        **more,
    )


def units_kernel(teacher_ref, student_ref, teacher_out, student_out):
    teacher, _ = unit_rows(teacher_ref[...])
    student, _ = unit_rows(student_ref[...])
    for chip in range(teacher_out.shape[0]):
        teacher_out[chip] = teacher.astype(jnp.bfloat16)
        student_out[chip] = student.astype(jnp.bfloat16)


def directions_kernel(block_ref, teacher_ref, student_ref, teacher_out, student_out, copy_out, inverse_out):
    teacher, _ = unit_columns(teacher_ref[...])
    teacher_out[...] = jnp.transpose(teacher).astype(jnp.bfloat16)
    student, length = unit_columns(student_ref[...])
    student_out[...] = jnp.transpose(student).astype(jnp.bfloat16)
    copy_out[...] = student_ref[...]
    inverse_out[...] = 1.0 / length


def in_crop_order(core, own_ref, other_ref, units_ref):
    chips, rows, _ = own_ref.shape
    for chip in range(chips):
        units_ref[pl.ds(pl.multiple_of((2 * chip + core) * rows, rows), rows), :] = own_ref[chip]
        units_ref[pl.ds(pl.multiple_of((2 * chip + 1 - core) * rows, rows), rows), :] = other_ref[chip]


def exponentials(directions, units, temperature):
    logits = lax.dot_general(
        directions, units, (((1,), (1,)), ((), ())), preferred_element_type=jnp.float32
    )
    return jnp.exp2(logits * (math.log2(math.e) / temperature))


def fold(values):
    rows, lanes = values.shape
    return jnp.sum(values.reshape(rows // 8, 8, lanes), axis=0)


def as_rows(line):
    return jnp.concatenate([line[:, at : at + LANES] for at in range(0, line.shape[1], LANES)], axis=0)


def as_line(rows):
    return jnp.concatenate([rows[at : at + 1, :] for at in range(rows.shape[0])], axis=1)


def send(sent_ref, total, *more):
    values = jnp.concatenate([as_rows(total), *more], axis=0).astype(jnp.bfloat16)
    for device in range(sent_ref.shape[0]):
        sent_ref[device] = values


def received(got_ref):
    total = got_ref[0].astype(jnp.float32)
    for device in range(1, got_ref.shape[0]):
        total = total + got_ref[device].astype(jnp.float32)
    return total


def teacher_kernel(prototypes, core_ref, directions_ref, own_ref, other_ref, weight_ref, mass_ref, sent_ref, units_ref, total_ref):
    in_crop_order(core_ref[0], own_ref, other_ref, units_ref)
    total_ref[...] = jnp.zeros_like(total_ref)

    @pl.loop(0, directions_ref.shape[0] // TILE)
    def _(step):
        here = pl.ds(pl.multiple_of(step * TILE, TILE), TILE)
        mass = exponentials(directions_ref[here, :], units_ref[...], teacher_temp)
        mass_ref[here, :] = mass
        scale = 1.0 / (prototypes * jnp.sum(mass, axis=1, keepdims=True))
        total_ref[...] += fold(mass * scale)

    send(sent_ref, jnp.sum(total_ref[...], axis=0, keepdims=True), weight_ref[...])


def student_kernel(core_ref, directions_ref, own_ref, other_ref, mass_ref, part_ref, turned_ref, units_ref, total_ref):
    in_crop_order(core_ref[0], own_ref, other_ref, units_ref)
    turned_ref[...] = jnp.transpose(units_ref[...].astype(jnp.float32)).astype(jnp.bfloat16)
    total_ref[...] = jnp.zeros_like(total_ref)

    @pl.loop(0, directions_ref.shape[0] // TILE)
    def _(step):
        here = pl.ds(pl.multiple_of(step * TILE, TILE), TILE)
        mass = exponentials(directions_ref[here, :], units_ref[...], student_temp)
        mass_ref[here, :] = mass
        total_ref[...] += fold(mass)

    part_ref[...] = as_rows(jnp.sum(total_ref[...], axis=0, keepdims=True))


def sweep_kernel(prototypes, crops, extra, mass_ref, got_ref, *refs):
    sent_ref, scale_ref, total_ref = refs[-3:]
    crop_scale = as_line(1.0 / (crops * received(got_ref)[: crops // LANES]))
    total_ref[...] = jnp.zeros_like(total_ref)

    @pl.loop(0, mass_ref.shape[0] // TILE)
    def _(step):
        here = pl.ds(pl.multiple_of(step * TILE, TILE), TILE)
        mass = mass_ref[here, :]
        scale = 1.0 / (prototypes * jnp.sum(mass * crop_scale, axis=1, keepdims=True))
        scale_ref[here, :] = scale
        total_ref[...] += fold(mass * scale)

    more = [refs[0][...]] if extra else []
    send(sent_ref, jnp.sum(total_ref[...], axis=0, keepdims=True), *more)


def gradient_kernel(
    core_ref, teacher_ref, student_ref, scale_ref, got_ref, crop_ref, turned_ref, copy_ref, inverse_ref,
    sent_ref, keep_ref, give_ref, gradient_ref, sum_ref,
):
    core = core_ref[0]
    chips, rows_each, _ = sent_ref.shape
    lines = student_ref.shape[1] // LANES
    totals = received(got_ref)
    weights = crop_ref[...] / student_temp
    teacher_scale = as_line(weights / totals[:lines])
    student_scale = as_line(weights / totals[lines:])
    sum_ref[...] = jnp.zeros_like(sum_ref)

    @pl.loop(0, student_ref.shape[0] // TILE)
    def _(step):
        here = pl.ds(pl.multiple_of(step * TILE, TILE), TILE)
        gradient = student_ref[here, :] * student_scale - teacher_ref[here, :] * scale_ref[here, :] * teacher_scale
        gradient_ref[...] = gradient.astype(jnp.bfloat16)
        weight_grad = lax.dot_general(
            turned_ref[...], gradient_ref[...], (((1,), (1,)), ((), ())), preferred_element_type=jnp.float32
        )
        inverse = inverse_ref[:, here]
        unit = copy_ref[:, here].astype(jnp.float32) * inverse
        dot = jnp.sum(unit * weight_grad, axis=0, keepdims=True)
        grad = (weight_grad - unit * dot) * inverse
        sent_ref[:, :, here] = grad.astype(jnp.bfloat16).reshape(chips, rows_each, TILE)
        sum_ref[...] += jnp.dot(
            unit.astype(jnp.bfloat16), gradient_ref[...], preferred_element_type=jnp.float32
        )

    for chip in range(chips):
        rows = keep_ref.shape[1]
        both = jnp.transpose(sum_ref[:, 2 * chip * rows : (2 * chip + 2) * rows])
        first, second = both[:rows], both[rows:]
        keep_ref[chip] = jnp.where(core == 0, first, second)
        give_ref[chip] = jnp.where(core == 0, second, first).astype(jnp.bfloat16)


def pair_kernel(keep_ref, other_ref, out_ref):
    out_ref[...] = (keep_ref[...] + other_ref[...].astype(jnp.float32)).astype(jnp.bfloat16)


def feature_kernel(got_ref, student_ref, out_ref):
    total = received(got_ref)
    hat, length = unit_rows(student_ref[...])
    out_ref[...] = (total - hat * jnp.sum(hat * total, axis=1, keepdims=True)) / length


def widen_kernel(got_ref, out_ref):
    out_ref[...] = got_ref[0].astype(jnp.float32)


def kernel_body(teacher_feat, student_feat, crop_weight, teacher_v, student_v):
    f32, bf16 = jnp.float32, jnp.bfloat16
    shape = jax.ShapeDtypeStruct
    chips, fsdp = lax.axis_size("dp"), lax.axis_size("fsdp")
    devices = chips * fsdp
    rows, width = teacher_feat.shape
    crops = rows * devices
    lines = crops // LANES
    kept = teacher_v.shape[1]
    prototypes = kept * fsdp
    count = kept // chips
    block = lax.axis_index("dp")
    core = lax.axis_index("fsdp")[None]
    elements = count * crops
    smem, vmem = pl.BlockSpec(memory_space=pltpu.SMEM), pl.BlockSpec(memory_space=pltpu.VMEM)

    def swap(values):
        return lax.ppermute(values, "fsdp", [(0, 1), (1, 0)])

    teacher_sent, student_sent = call(
        units_kernel, (shape((chips, rows, width), bf16), shape((chips, rows, width), bf16))
    )(teacher_feat, student_feat)
    teacher_own = lax.all_to_all(teacher_sent, "dp", 0, 0)
    teacher_other = swap(teacher_own)
    student_own = lax.all_to_all(student_sent, "dp", 0, 0)
    student_other = swap(student_own)
    weights = jnp.pad(crop_weight[None, :].astype(f32), ((0, 7), (0, LANES - rows)))

    tiles = count // TILE
    column = pl.BlockSpec((width, TILE), lambda step, at: (0, at[0] * tiles + step))
    turned = pl.BlockSpec((TILE, width), lambda step, at: (step, 0))
    straight = pl.BlockSpec((width, TILE), lambda step, at: (0, step))
    line = pl.BlockSpec((1, TILE), lambda step, at: (0, step))
    teacher_w, student_w, student_copy, inverse = call(
        directions_kernel,
        (
            shape((count, width), bf16),
            shape((count, width), bf16),
            shape((width, count), bf16),
            shape((1, count), f32),
        ),
        flops=12 * count * width,
        moved=10 * count * width,
        grid_spec=pltpu.PrefetchScalarGridSpec(
            num_scalar_prefetch=1,
            grid=(tiles,),
            in_specs=[column, column],
            out_specs=[turned, turned, straight, line],
        ),
    )(
        block[None],
        pltpu.with_memory_space_constraint(teacher_v, pltpu.HBM),
        pltpu.with_memory_space_constraint(student_v, pltpu.HBM),
    )

    units = pltpu.VMEM((crops, width), bf16)
    total = pltpu.VMEM((8, crops), f32)
    mass, sent = call(
        functools.partial(teacher_kernel, prototypes),
        (pltpu.VMEM((count, crops), f32), shape((devices, lines + 8, LANES), bf16)),
        flops=2 * elements * width,
        exps=elements,
        in_specs=[smem] + [vmem] * 4,
        scratch_shapes=[units, total],
    )(core, teacher_w, teacher_own, teacher_other, weights)
    got = lax.all_to_all(sent, EVERY, 0, 0)
    crop_rows = got[:, lines, :rows].astype(f32).reshape(lines, LANES)

    student_mass, student_part, student_turned = call(
        student_kernel,
        (pltpu.VMEM((count, crops), f32), shape((lines, LANES), f32), shape((width, crops), bf16)),
        flops=2 * elements * width,
        exps=elements,
        in_specs=[smem] + [vmem] * 3,
        scratch_shapes=[units, total],
    )(core, student_w, student_own, student_other)

    for sweep in range(1, ITERS):
        extra = sweep == ITERS - 1
        sent, scale = call(
            functools.partial(sweep_kernel, prototypes, crops, extra),
            (shape((devices, lines * (1 + extra), LANES), bf16), shape((count, 1), f32)),
            flops=4 * elements,
            scratch_shapes=[total],
        )(mass, got, *([student_part] if extra else []))
        got = lax.all_to_all(sent, EVERY, 0, 0)

    out_rows = width // chips
    sent, keep, give = call(
        gradient_kernel,
        (
            shape((chips, out_rows, count), bf16),
            shape((chips, rows, width), f32),
            shape((chips, rows, width), bf16),
        ),
        flops=4 * elements * width,
        in_specs=[smem] + [vmem] * 8,
        scratch_shapes=[pltpu.VMEM((TILE, crops), bf16), pltpu.VMEM((width, crops), f32)],
    )(core, mass, student_mass, scale, got, crop_rows, student_turned, student_copy, inverse)
    grad_got = lax.all_to_all(sent, "dp", 0, 0)
    paired = call(pair_kernel, shape((chips, rows, width), bf16))(keep, swap(give))
    feature_got = lax.all_to_all(paired, "dp", 0, 0)
    grad_feat = call(feature_kernel, shape((rows, width), f32))(feature_got, student_feat)
    grad_v = call(
        widen_kernel,
        shape((out_rows, kept), f32),
        grid=(chips,),
        in_specs=[pl.BlockSpec((1, out_rows, count), lambda step: (step, 0, 0))],
        out_specs=pl.BlockSpec((out_rows, count), lambda step: (0, step)),
    )(grad_got)
    return (grad_v, grad_feat)


def solution(mesh):
    dp, fsdp = mesh.shape["dp"], mesh.shape["fsdp"]

    def run(teacher_feat, student_feat, crop_weight, teacher_v, student_v):
        crops = teacher_feat.shape[0]
        count = teacher_v.shape[1] // (dp * fsdp)
        fits = fsdp == 2 and count % TILE == 0 and crops % 1024 == 0 and 8 * count * crops <= KEPT_BYTES
        every = P(EVERY)
        return jax.shard_map(
            kernel_body if fits else plain_body,
            mesh=mesh,
            in_specs=(every, every, every, P(None, "fsdp"), P(None, "fsdp")),
            out_specs=(P("dp", "fsdp"), every),
            check_vma=False,
        )(teacher_feat, student_feat, crop_weight, teacher_v, student_v)

    return run
```

profile of v0, /device:TPU:0, one launch (start us, length us, event | category | flops | bytes accessed | tf_op | source)
XLA Modules:
  0.0 120.2 jit_solution(18422097852363199878)
XLA Ops:
  0.6 0.0 copy-start.6
  0.6 0.7 copy-done.6
  1.3 0.0 copy-start.8
  1.4 0.7 copy-done.8
  2.1 0.8 shard_map.69
  2.9 18.0 %all_to_all.35.own_ref = bf16[16,32,256]{2,1,0:T(8,128)(2,1)S(1)} all-to-all(bf16[16,32,256]{2,1,0:T(8,128)(2,1)S(1)} %get-tuple-element.20), channel_id=1, replica_groups=mesh['dp'=16,'fsdp'=2] {'dp'}, dimensions={0} | all-to-all | bytes 524288 | tf_op jit(solution)/shard_map/all_to_all | solution.py:310
  20.9 3.5 %all-to-all-start.1 = ((bf16[16,32,256]{2,1,0:T(8,128)(2,1)}), bf16[16,32,256]{2,1,0:T(8,128)(2,1)S(1)}, u32[]{:S(2)}, u32[]{:S(2)}) async-start(bf16[16,32,256]{2,1,0:T(8,128)(2,1)} %get-tuple-element.23), calls=%async_computation.1 | async-start | bytes 524288 | tf_op jit(solution)/shard_map/all_to_all | solution.py:312
  24.4 0.1 collective-permute-start
  24.5 0.0 copy-start.9
  24.5 2.7 %shard_map.68 = (bf16[1024,256]{1,0:T(8,128)(2,1)S(1)}, bf16[1024,256]{1,0:T(8,128)(2,1)S(1)}, bf16[256,1024]{1,0:T(8,128)(2,1)S(1)}, f32[1,1024]{1,0:T(1,128)S(1)}) custom-call(s32[1]{0:T(128)} %bitcast.1.block_ref, bf16[256,16384]{1,0:T(8,128)(2,1)} %teacher_ref.2, bf16[256,16384]{1,0:T(8,128)(2,1)} %student_ref.3), custom_call_target="tpu_custom_call" | custom-call | flops 3145728 | bytes 2621440 | tf_op jit(solution)/shard_map/pallas_call | solution.py:321
  27.2 0.0 copy-done.9
  27.2 0.0 collective-permute-done.other_ref
  27.2 2.5 %shard_map.70 = (f32[1024,1024]{1,0:T(8,128)S(1)}, bf16[32,16,128]{2,1,0:T(8,128)(2,1)}) custom-call(s32[1]{0:T(128)} %bitcast.core_ref, bf16[1024,256]{1,0:T(8,128)(2,1)S(1)} %get-tuple-element.19.directions_ref, bf16[16,32,256]{2,1,0:T(8,128)(2,1)S(1)} %all_to_all.35.own_ref, bf16[16,32,256]{2,1,0:T(8,128)(2,1)S(1)} %collective-permute-done.other_ref, ...), custom_call_target="tpu_custom_call" | custom-call | flops 536870912 | tf_op jit(solution)/shard_map/pallas_call | solution.py:345
  29.7 0.0 copy-start
  29.7 1.9 %copy-done = f32[1024,1024]{1,0:T(8,128)} copy-done((f32[1024,1024]{1,0:T(8,128)}, f32[1024,1024]{1,0:T(8,128)S(1)}, u32[]{:S(2)}) %copy-start) | copy-done | bytes 4194328
  31.7 2.0 %all-to-all-done.1.own_ref = bf16[16,32,256]{2,1,0:T(8,128)(2,1)S(1)} async-done(((bf16[16,32,256]{2,1,0:T(8,128)(2,1)}), bf16[16,32,256]{2,1,0:T(8,128)(2,1)S(1)}, u32[]{:S(2)}, u32[]{:S(2)}) %all-to-all-start.1) | async-done | bytes 262176 | tf_op jit(solution)/shard_map/all_to_all | solution.py:312
  33.6 3.9 %all-to-all-start.2 = ((bf16[32,16,128]{2,1,0:T(8,128)(2,1)}), bf16[32,16,128]{2,1,0:T(8,128)(2,1)S(1)}, u32[]{:S(2)}, u32[]{:S(2)}) async-start(bf16[32,16,128]{2,1,0:T(8,128)(2,1)} %get-tuple-element.25), calls=%async_computation.2 | async-start | bytes 262144 | tf_op jit(solution)/shard_map/all_to_all | solution.py:353
  37.6 0.3 collective-permute-start.1
  37.9 7.9 %all-to-all-done.2.got_ref = bf16[32,16,128]{2,1,0:T(8,128)(2,1)S(1)} async-done(((bf16[32,16,128]{2,1,0:T(8,128)(2,1)}), bf16[32,16,128]{2,1,0:T(8,128)(2,1)S(1)}, u32[]{:S(2)}, u32[]{:S(2)}) %all-to-all-start.2) | async-done | bytes 131104 | tf_op jit(solution)/shard_map/all_to_all | solution.py:353
  45.8 0.0 copy-start.1
  45.8 2.2 %copy-done.1 = f32[1024,1024]{1,0:T(8,128)S(1)} copy-done((f32[1024,1024]{1,0:T(8,128)S(1)}, f32[1024,1024]{1,0:T(8,128)}, u32[]{:S(2)}) %copy-start.1) | copy-done | bytes 4194328
  48.0 1.5 %shard_map.72 = (bf16[32,8,128]{2,1,0:T(8,128)(2,1)}, f32[1024,1]{1,0:T(8,128)}) custom-call(f32[1024,1024]{1,0:T(8,128)S(1)} %copy-done.1, bf16[32,16,128]{2,1,0:T(8,128)(2,1)S(1)} %all-to-all-done.2.got_ref), custom_call_target="tpu_custom_call" | custom-call | flops 4194304 | tf_op jit(solution)/shard_map/pallas_call | solution.py:367
  49.5 2.6 %all-to-all-start.3 = ((bf16[32,8,128]{2,1,0:T(8,128)(2,1)}), bf16[32,8,128]{2,1,0:T(8,128)(2,1)S(1)}, u32[]{:S(2)}, u32[]{:S(2)}) async-start(bf16[32,8,128]{2,1,0:T(8,128)(2,1)} %get-tuple-element.26), calls=%async_computation.3 | async-start | bytes 131072 | tf_op jit(solution)/shard_map/all_to_all | solution.py:373
  52.1 0.0 collective-permute-done.1.other_ref
  52.1 1.6 %shard_map.71 = (f32[1024,1024]{1,0:T(8,128)S(1)}, f32[8,128]{1,0:T(8,128)S(1)}, bf16[256,1024]{1,0:T(8,128)(2,1)S(1)}) custom-call(s32[1]{0:T(128)} %bitcast.core_ref, bf16[1024,256]{1,0:T(8,128)(2,1)S(1)} %get-tuple-element.22.directions_ref, bf16[16,32,256]{2,1,0:T(8,128)(2,1)S(1)} %all-to-all-done.1.own_ref, ...), custom_call_target="tpu_custom_call" | custom-call | flops 536870912 | tf_op jit(solution)/shard_map/pallas_call | solution.py:356
  53.7 0.0 copy-start.4
  53.8 2.0 %copy-done.4 = f32[1024,1024]{1,0:T(8,128)} copy-done((f32[1024,1024]{1,0:T(8,128)}, f32[1024,1024]{1,0:T(8,128)S(1)}, u32[]{:S(2)}) %copy-start.4) | copy-done | bytes 4194328
  55.8 3.7 %all-to-all-done.3.got_ref = bf16[32,8,128]{2,1,0:T(8,128)(2,1)S(1)} async-done(((bf16[32,8,128]{2,1,0:T(8,128)(2,1)}), bf16[32,8,128]{2,1,0:T(8,128)(2,1)S(1)}, u32[]{:S(2)}, u32[]{:S(2)}) %all-to-all-start.3) | async-done | bytes 65568 | tf_op jit(solution)/shard_map/all_to_all | solution.py:373
  59.5 0.0 copy-start.2
  59.5 2.2 %copy-done.2 = f32[1024,1024]{1,0:T(8,128)S(1)} copy-done((f32[1024,1024]{1,0:T(8,128)S(1)}, f32[1024,1024]{1,0:T(8,128)}, u32[]{:S(2)}) %copy-start.2) | copy-done | bytes 4194328
  61.7 0.0 copy-start.7
  61.7 1.4 %shard_map.73 = (bf16[32,16,128]{2,1,0:T(8,128)(2,1)}, f32[1024,1]{1,0:T(8,128)S(1)}) custom-call(f32[1024,1024]{1,0:T(8,128)S(1)} %copy-done.2, bf16[32,8,128]{2,1,0:T(8,128)(2,1)S(1)} %all-to-all-done.3.got_ref, f32[8,128]{1,0:T(8,128)S(1)} %get-tuple-element.27.refs_0_), custom_call_target="tpu_custom_call" | custom-call | flops 4194304 | tf_op jit(solution)/shard_map/pallas_call | solution.py:367
  63.1 2.6 %all-to-all-start.4 = ((bf16[32,16,128]{2,1,0:T(8,128)(2,1)}), bf16[32,16,128]{2,1,0:T(8,128)(2,1)S(1)}, u32[]{:S(2)}, u32[]{:S(2)}) async-start(bf16[32,16,128]{2,1,0:T(8,128)(2,1)} %get-tuple-element.29), calls=%async_computation.4 | async-start | bytes 262144 | tf_op jit(solution)/shard_map/all_to_all | solution.py:373
  65.8 0.1 reshape.10.crop_ref
  65.8 8.1 %all-to-all-done.4.got_ref = bf16[32,16,128]{2,1,0:T(8,128)(2,1)S(1)} async-done(((bf16[32,16,128]{2,1,0:T(8,128)(2,1)}), bf16[32,16,128]{2,1,0:T(8,128)(2,1)S(1)}, u32[]{:S(2)}, u32[]{:S(2)}) %all-to-all-start.4) | async-done | bytes 131104 | tf_op jit(solution)/shard_map/all_to_all | solution.py:373
  73.9 0.0 copy-start.3
  73.9 2.2 %copy-done.3 = f32[1024,1024]{1,0:T(8,128)S(1)} copy-done((f32[1024,1024]{1,0:T(8,128)S(1)}, f32[1024,1024]{1,0:T(8,128)}, u32[]{:S(2)}) %copy-start.3) | copy-done | bytes 4194328
  76.1 0.0 copy-start.5
  76.1 2.2 %copy-done.5 = f32[1024,1024]{1,0:T(8,128)S(1)} copy-done((f32[1024,1024]{1,0:T(8,128)S(1)}, f32[1024,1024]{1,0:T(8,128)}, u32[]{:S(2)}) %copy-start.5) | copy-done | bytes 4194328
  78.3 3.9 %shard_map.74 = (bf16[16,16,1024]{2,1,0:T(8,128)(2,1)}, f32[16,32,256]{2,1,0:T(8,128)S(1)}, bf16[16,32,256]{2,1,0:T(8,128)(2,1)S(1)}) custom-call(s32[1]{0:T(128)} %bitcast.core_ref, f32[1024,1024]{1,0:T(8,128)S(1)} %copy-done.3, f32[1024,1024]{1,0:T(8,128)S(1)} %copy-done.5, f32[1024,1]{1,0:T(8,128)S(1)} %get-tuple-element.28.scale_ref, ...), custom_call_target="tpu_custom_call" | custom-call | flops 1073741824 | tf_op jit(solution)/shard_map/pallas_call | solution.py:376
  82.2 0.2 collective-permute-start.2
  82.4 1.3 %collective-permute-done.2.other_ref = bf16[16,32,256]{2,1,0:T(8,128)(2,1)S(1)} collective-permute-done((bf16[16,32,256]{2,1,0:T(8,128)(2,1)S(1)}, bf16[16,32,256]{2,1,0:T(8,128)(2,1)S(1)}, u32[]{:S(2)}, u32[]{:S(2)}) %collective-permute-start.2) | collective-permute-done | bytes 262176 | tf_op jit(solution)/shard_map/ppermute | solution.py:305
  83.8 13.1 %all_to_all.36.got_ref = bf16[16,32,256]{2,1,0:T(8,128)(2,1)S(1)} all-to-all(bf16[16,32,256]{2,1,0:T(8,128)(2,1)S(1)} %shard_map.76), channel_id=1, replica_groups=mesh['dp'=16,'fsdp'=2] {'dp'}, dimensions={0} | all-to-all | bytes 524288 | tf_op jit(solution)/shard_map/all_to_all | solution.py:389
  96.9 3.6 %all-to-all-start.5 = ((bf16[16,16,1024]{2,1,0:T(8,128)(2,1)}), bf16[16,16,1024]{2,1,0:T(8,128)(2,1)S(1)}, u32[]{:S(2)}, u32[]{:S(2)}) async-start(bf16[16,16,1024]{2,1,0:T(8,128)(2,1)} %get-tuple-element.33), calls=%async_computation.5 | async-start | bytes 1048576 | tf_op jit(solution)/shard_map/all_to_all | solution.py:387
  100.5 0.0 copy-done.7
  100.5 0.8 shard_map.77
  101.3 13.8 %all-to-all-done.5.got_ref = bf16[16,16,1024]{2,1,0:T(8,128)(2,1)S(1)} async-done(((bf16[16,16,1024]{2,1,0:T(8,128)(2,1)}), bf16[16,16,1024]{2,1,0:T(8,128)(2,1)S(1)}, u32[]{:S(2)}, u32[]{:S(2)}) %all-to-all-start.5) | async-done | bytes 524320 | tf_op jit(solution)/shard_map/all_to_all | solution.py:387
  115.1 5.1 %shard_map.75 = f32[16,16384]{1,0:T(8,128)} custom-call(bf16[16,16,1024]{2,1,0:T(8,128)(2,1)S(1)} %all-to-all-done.5.got_ref), custom_call_target="tpu_custom_call" | custom-call | tf_op jit(solution)/shard_map/pallas_call | solution.py:391
  (3 shorter events, 0.1 us)
Async XLA Ops:
  0.6 0.7 copy-start.6
  1.3 0.7 copy-start.8
  20.9 12.8 %all-to-all-start.1 = ((bf16[16,32,256]{2,1,0:T(8,128)(2,1)}), bf16[16,32,256]{2,1,0:T(8,128)(2,1)S(1)}, u32[]{:S(2)}, u32[]{:S(2)}) async-start(bf16[16,32,256]{2,1,0:T(8,128)(2,1)} %get-tuple-element.23), calls=%async_computation.1 | async-start | bytes 524288 | tf_op jit(solution)/shard_map/all_to_all | solution.py:312
  24.4 2.8 %collective-permute-start = (bf16[16,32,256]{2,1,0:T(8,128)(2,1)S(1)}, bf16[16,32,256]{2,1,0:T(8,128)(2,1)S(1)}, u32[]{:S(2)}, u32[]{:S(2)}) collective-permute-start(bf16[16,32,256]{2,1,0:T(8,128)(2,1)S(1)} %all_to_all.35.own_ref), channel_id=1, source_target_pairs={{0,1},{1,0},{2,3},{3,2},{4,5},{5,4},{6,7},{7,6},{8,9},{9,8},{10,11... | collective-permute-start | bytes 786440 | tf_op jit(solution)/shard_map/ppermute | solution.py:305
  24.5 2.7 %copy-start.9 = (bf16[32]{0:T(256)(128)(2,1)S(1)}, bf16[32]{0:T(256)(128)(2,1)}, u32[]{:S(2)}) copy-start(bf16[32]{0:T(256)(128)(2,1)} %param.7) | copy-start | bytes 196
  29.7 1.9 %copy-start = (f32[1024,1024]{1,0:T(8,128)}, f32[1024,1024]{1,0:T(8,128)S(1)}, u32[]{:S(2)}) copy-start(f32[1024,1024]{1,0:T(8,128)S(1)} %get-tuple-element.21.mass_ref.teacher_ref) | copy-start | bytes 12582916
  33.6 12.2 %all-to-all-start.2 = ((bf16[32,16,128]{2,1,0:T(8,128)(2,1)}), bf16[32,16,128]{2,1,0:T(8,128)(2,1)S(1)}, u32[]{:S(2)}, u32[]{:S(2)}) async-start(bf16[32,16,128]{2,1,0:T(8,128)(2,1)} %get-tuple-element.25), calls=%async_computation.2 | async-start | bytes 262144 | tf_op jit(solution)/shard_map/all_to_all | solution.py:353
  37.6 14.5 %collective-permute-start.1 = (bf16[16,32,256]{2,1,0:T(8,128)(2,1)S(1)}, bf16[16,32,256]{2,1,0:T(8,128)(2,1)S(1)}, u32[]{:S(2)}, u32[]{:S(2)}) collective-permute-start(bf16[16,32,256]{2,1,0:T(8,128)(2,1)S(1)} %all-to-all-done.1.own_ref), channel_id=1, source_target_pairs={{0,1},{1,0},{2,3},{3,2},{4,5},{5,4},{6,7},{7,6},{8,9},{9,8},{10,11... | collective-permute-start | bytes 786440 | tf_op jit(solution)/shard_map/ppermute | solution.py:305
  45.8 2.2 %copy-start.1 = (f32[1024,1024]{1,0:T(8,128)S(1)}, f32[1024,1024]{1,0:T(8,128)}, u32[]{:S(2)}) copy-start(f32[1024,1024]{1,0:T(8,128)} %copy-done) | copy-start | bytes 12582916
  49.5 10.0 %all-to-all-start.3 = ((bf16[32,8,128]{2,1,0:T(8,128)(2,1)}), bf16[32,8,128]{2,1,0:T(8,128)(2,1)S(1)}, u32[]{:S(2)}, u32[]{:S(2)}) async-start(bf16[32,8,128]{2,1,0:T(8,128)(2,1)} %get-tuple-element.26), calls=%async_computation.3 | async-start | bytes 131072 | tf_op jit(solution)/shard_map/all_to_all | solution.py:373
  53.7 2.0 %copy-start.4 = (f32[1024,1024]{1,0:T(8,128)}, f32[1024,1024]{1,0:T(8,128)S(1)}, u32[]{:S(2)}) copy-start(f32[1024,1024]{1,0:T(8,128)S(1)} %get-tuple-element.24.student_ref) | copy-start | bytes 12582916
  59.5 2.2 %copy-start.2 = (f32[1024,1024]{1,0:T(8,128)S(1)}, f32[1024,1024]{1,0:T(8,128)}, u32[]{:S(2)}) copy-start(f32[1024,1024]{1,0:T(8,128)} %copy-done) | copy-start | bytes 12582916
  61.7 38.8 %copy-start.7 = (bf16[32,256]{1,0:T(8,128)(2,1)S(1)}, bf16[32,256]{1,0:T(8,128)(2,1)}, u32[]{:S(2)}) copy-start(bf16[32,256]{1,0:T(8,128)(2,1)} %student_ref.5) | copy-start | bytes 49156
  63.1 10.8 %all-to-all-start.4 = ((bf16[32,16,128]{2,1,0:T(8,128)(2,1)}), bf16[32,16,128]{2,1,0:T(8,128)(2,1)S(1)}, u32[]{:S(2)}, u32[]{:S(2)}) async-start(bf16[32,16,128]{2,1,0:T(8,128)(2,1)} %get-tuple-element.29), calls=%async_computation.4 | async-start | bytes 262144 | tf_op jit(solution)/shard_map/all_to_all | solution.py:373
  73.9 2.2 %copy-start.3 = (f32[1024,1024]{1,0:T(8,128)S(1)}, f32[1024,1024]{1,0:T(8,128)}, u32[]{:S(2)}) copy-start(f32[1024,1024]{1,0:T(8,128)} %copy-done) | copy-start | bytes 12582916
  76.1 2.2 %copy-start.5 = (f32[1024,1024]{1,0:T(8,128)S(1)}, f32[1024,1024]{1,0:T(8,128)}, u32[]{:S(2)}) copy-start(f32[1024,1024]{1,0:T(8,128)} %copy-done.4) | copy-start | bytes 12582916
  82.2 1.5 %collective-permute-start.2 = (bf16[16,32,256]{2,1,0:T(8,128)(2,1)S(1)}, bf16[16,32,256]{2,1,0:T(8,128)(2,1)S(1)}, u32[]{:S(2)}, u32[]{:S(2)}) collective-permute-start(bf16[16,32,256]{2,1,0:T(8,128)(2,1)S(1)} %get-tuple-element.35), channel_id=1, source_target_pairs={{0,1},{1,0},{2,3},{3,2},{4,5},{5,4},{6,7},{7,6},{8,9},{9,8},{10,11... | collective-permute-start | bytes 786440 | tf_op jit(solution)/shard_map/ppermute | solution.py:305
  96.9 18.2 %all-to-all-start.5 = ((bf16[16,16,1024]{2,1,0:T(8,128)(2,1)}), bf16[16,16,1024]{2,1,0:T(8,128)(2,1)S(1)}, u32[]{:S(2)}, u32[]{:S(2)}) async-start(bf16[16,16,1024]{2,1,0:T(8,128)(2,1)} %get-tuple-element.33), calls=%async_computation.5 | async-start | bytes 1048576 | tf_op jit(solution)/shard_map/all_to_all | solution.py:387
where the time goes:
time: 121 us; the launch traced here: 120 us
  waiting for transfers between devices  36.9 us (30%)
  blocking collectives  31.1 us (26%)
  Pallas kernels  20.4 us (17%)
  starting transfers between devices  16.8 us (14%)
  local copies, waits for them, and re-layouts  14.2 us (12%)
    all_to_all x3, waiting for transfers between devices, kernel_body(): got = lax.all_to_all(sent, EVERY, 0, 0)  19.7 us
    all_to_all x1, blocking collectives, kernel_body(): teacher_own = lax.all_to_all(teacher_sent, 'dp', 0, 0)  18 us
    unnamed x20, local copies, waits for them, and re-layouts  14.2 us
    all_to_all x1, waiting for transfers between devices, kernel_body(): grad_got = lax.all_to_all(sent, 'dp', 0, 0)  13.8 us
    all_to_all x1, blocking collectives, kernel_body(): feature_got = lax.all_to_all(paired, 'dp', 0, 0)  13.1 us
    all_to_all x3, starting transfers between devices, kernel_body(): got = lax.all_to_all(sent, EVERY, 0, 0)  9.06 us
    pallas_call x1, Pallas kernels, kernel_body(): call(widen_kernel, shape((out_rows, kept), f32), grid=(chips,), in_specs=...  5.09 us
    pallas_call x1, Pallas kernels, kernel_body(): call(gradient_kernel, (shape((chips, out_rows, count), bf16), shape((chip...  3.9 us
  transfers between devices with their start and end apart: 8, of which 6 were waited for; matrix products, arithmetic and copies ran while one was open for 0% of the time, Pallas kernels for 8%

commit v1 on v0

--- a/solution.py
+++ b/solution.py
@@ -16,6 +16,7 @@
 
 TILE = 256
 LANES = 128
+PLANE = 4
 VMEM_BYTES = 24 << 20
 KEPT_BYTES = 16 << 20
 
@@ -130,11 +131,8 @@
 
 
 def units_kernel(teacher_ref, student_ref, teacher_out, student_out):
-    teacher, _ = unit_rows(teacher_ref[...])
-    student, _ = unit_rows(student_ref[...])
-    for chip in range(teacher_out.shape[0]):
-        teacher_out[chip] = teacher.astype(jnp.bfloat16)
-        student_out[chip] = student.astype(jnp.bfloat16)
+    teacher_out[...] = unit_rows(teacher_ref[...])[0].astype(jnp.bfloat16)
+    student_out[...] = unit_rows(student_ref[...])[0].astype(jnp.bfloat16)
 
 
 def directions_kernel(block_ref, teacher_ref, student_ref, teacher_out, student_out, copy_out, inverse_out):
@@ -146,11 +144,15 @@
     inverse_out[...] = 1.0 / length
 
 
-def in_crop_order(core, own_ref, other_ref, units_ref):
-    chips, rows, _ = own_ref.shape
-    for chip in range(chips):
-        units_ref[pl.ds(pl.multiple_of((2 * chip + core) * rows, rows), rows), :] = own_ref[chip]
-        units_ref[pl.ds(pl.multiple_of((2 * chip + 1 - core) * rows, rows), rows), :] = other_ref[chip]
+def in_crop_order(chip, core, layers, got_refs, units_ref):
+    layer, place = chip // PLANE, chip % PLANE
+    for index, got_ref in enumerate(got_refs):
+        other, move = divmod(index, PLANE)
+        rows = got_ref.shape[0] // layers
+        for back in range(layers):
+            device = 2 * (((layer + layers - back) % layers) * PLANE + (place ^ move)) + (core ^ other)
+            here = pl.ds(pl.multiple_of(device * rows, rows), rows)
+            units_ref[here, :] = got_ref[back * rows : (back + 1) * rows, :]
 
 
 def exponentials(directions, units, temperature):
@@ -173,21 +175,16 @@
     return jnp.concatenate([rows[at : at + 1, :] for at in range(rows.shape[0])], axis=1)
 
 
-def send(sent_ref, total, *more):
-    values = jnp.concatenate([as_rows(total), *more], axis=0).astype(jnp.bfloat16)
-    for device in range(sent_ref.shape[0]):
-        sent_ref[device] = values
-
-
-def received(got_ref):
-    total = got_ref[0].astype(jnp.float32)
-    for device in range(1, got_ref.shape[0]):
-        total = total + got_ref[device].astype(jnp.float32)
+def added(refs):
+    total = refs[0][...].astype(jnp.float32)
+    for ref in refs[1:]:
+        total = total + ref[...].astype(jnp.float32)
     return total
 
 
-def teacher_kernel(prototypes, core_ref, directions_ref, own_ref, other_ref, weight_ref, mass_ref, sent_ref, units_ref, total_ref):
-    in_crop_order(core_ref[0], own_ref, other_ref, units_ref)
+def teacher_kernel(prototypes, layers, place_ref, directions_ref, *refs):
+    *got_refs, weight_ref, mass_ref, sent_ref, units_ref, total_ref = refs
+    in_crop_order(place_ref[0], place_ref[1], layers, got_refs, units_ref)
     total_ref[...] = jnp.zeros_like(total_ref)
 
     @pl.loop(0, directions_ref.shape[0] // TILE)
@@ -198,11 +195,14 @@
         scale = 1.0 / (prototypes * jnp.sum(mass, axis=1, keepdims=True))
         total_ref[...] += fold(mass * scale)
 
-    send(sent_ref, jnp.sum(total_ref[...], axis=0, keepdims=True), weight_ref[...])
-
-
-def student_kernel(core_ref, directions_ref, own_ref, other_ref, mass_ref, part_ref, turned_ref, units_ref, total_ref):
-    in_crop_order(core_ref[0], own_ref, other_ref, units_ref)
+    lines = weight_ref.shape[0]
+    sent_ref[:lines, :] = as_rows(jnp.sum(total_ref[...], axis=0, keepdims=True))
+    sent_ref[lines:, :] = weight_ref[...]
+
+
+def student_kernel(layers, place_ref, directions_ref, *refs):
+    *got_refs, mass_ref, part_ref, turned_ref, units_ref, total_ref = refs
+    in_crop_order(place_ref[0], place_ref[1], layers, got_refs, units_ref)
     turned_ref[...] = jnp.transpose(units_ref[...].astype(jnp.float32)).astype(jnp.bfloat16)
     total_ref[...] = jnp.zeros_like(total_ref)
 
@@ -216,9 +216,11 @@
     part_ref[...] = as_rows(jnp.sum(total_ref[...], axis=0, keepdims=True))
 
 
-def sweep_kernel(prototypes, crops, extra, mass_ref, got_ref, *refs):
+def sweep_kernel(prototypes, crops, layers, mass_ref, *refs):
+    part_refs = refs[layers:-3]
     sent_ref, scale_ref, total_ref = refs[-3:]
-    crop_scale = as_line(1.0 / (crops * received(got_ref)[: crops // LANES]))
+    lines = crops // LANES
+    crop_scale = as_line(1.0 / (crops * added(refs[:layers])[:lines]))
     total_ref[...] = jnp.zeros_like(total_ref)
 
     @pl.loop(0, mass_ref.shape[0] // TILE)
@@ -229,19 +231,19 @@
         scale_ref[here, :] = scale
         total_ref[...] += fold(mass * scale)
 
-    more = [refs[0][...]] if extra else []
-    send(sent_ref, jnp.sum(total_ref[...], axis=0, keepdims=True), *more)
-
-
-def gradient_kernel(
-    core_ref, teacher_ref, student_ref, scale_ref, got_ref, crop_ref, turned_ref, copy_ref, inverse_ref,
-    sent_ref, keep_ref, give_ref, gradient_ref, sum_ref,
-):
-    core = core_ref[0]
-    chips, rows_each, _ = sent_ref.shape
+    sent_ref[:lines, :] = as_rows(jnp.sum(total_ref[...], axis=0, keepdims=True))
+    for part_ref in part_refs:
+        sent_ref[lines:, :] = part_ref[...]
+
+
+def gradient_kernel(layers, chips, place_ref, teacher_ref, student_ref, scale_ref, turned_ref, copy_ref, inverse_ref, *refs):
+    total_refs, crop_refs, refs = refs[:layers], refs[layers : 2 * layers], refs[2 * layers :]
+    sent_refs, (keep_ref, give_ref, gradient_ref, grad_ref, sum_ref) = refs[:chips], refs[chips:]
+    chip, core = place_ref[0], place_ref[1]
+    rows_each = sent_refs[0].shape[0]
     lines = student_ref.shape[1] // LANES
-    totals = received(got_ref)
-    weights = crop_ref[...] / student_temp
+    totals = added(total_refs)
+    weights = added(crop_refs)[lines:] / student_temp
     teacher_scale = as_line(weights / totals[:lines])
     student_scale = as_line(weights / totals[lines:])
     sum_ref[...] = jnp.zeros_like(sum_ref)
@@ -257,32 +259,57 @@
         inverse = inverse_ref[:, here]
         unit = copy_ref[:, here].astype(jnp.float32) * inverse
         dot = jnp.sum(unit * weight_grad, axis=0, keepdims=True)
-        grad = (weight_grad - unit * dot) * inverse
-        sent_ref[:, :, here] = grad.astype(jnp.bfloat16).reshape(chips, rows_each, TILE)
+        grad_ref[...] = (weight_grad - unit * dot) * inverse
+        for move in range(chips):
+            rows = pl.ds(pl.multiple_of((chip ^ move) * rows_each, rows_each), rows_each)
+            sent_refs[move][:, here] = grad_ref[rows, :].astype(jnp.bfloat16)
         sum_ref[...] += jnp.dot(
             unit.astype(jnp.bfloat16), gradient_ref[...], preferred_element_type=jnp.float32
         )
 
-    for chip in range(chips):
-        rows = keep_ref.shape[1]
-        both = jnp.transpose(sum_ref[:, 2 * chip * rows : (2 * chip + 2) * rows])
+    rows = keep_ref.shape[2]
+    for source in range(chips):
+        layer, place = divmod(source, PLANE)
+        both = jnp.transpose(sum_ref[:, 2 * source * rows : (2 * source + 2) * rows])
         first, second = both[:rows], both[rows:]
-        keep_ref[chip] = jnp.where(core == 0, first, second)
-        give_ref[chip] = jnp.where(core == 0, second, first).astype(jnp.bfloat16)
-
-
-def pair_kernel(keep_ref, other_ref, out_ref):
-    out_ref[...] = (keep_ref[...] + other_ref[...].astype(jnp.float32)).astype(jnp.bfloat16)
-
-
-def feature_kernel(got_ref, student_ref, out_ref):
-    total = received(got_ref)
+        move = (chip % PLANE) ^ place
+        keep_ref[move, layer] = jnp.where(core == 0, first, second)
+        give_ref[move, layer] = jnp.where(core == 0, second, first).astype(jnp.bfloat16)
+
+
+def pair_kernel(keep_ref, other_ref, own_out, *out_refs):
+    own_out[...] = keep_ref[0] + other_ref[0].astype(jnp.float32)
+    for move, out_ref in enumerate(out_refs, 1):
+        out_ref[...] = (keep_ref[move] + other_ref[move].astype(jnp.float32)).astype(jnp.bfloat16)
+
+
+def plane_kernel(place_ref, *refs):
+    got_refs, (own_out, *out_refs) = refs[:PLANE], refs[PLANE:]
+    layers = got_refs[0].shape[0]
+    layer = place_ref[0] // PLANE
+    for back in range(layers):
+        at = (layer + layers - back) % layers
+        total = got_refs[0][at]
+        for got_ref in got_refs[1:]:
+            total = total + got_ref[at].astype(jnp.float32)
+        if back == 0:
+            own_out[...] = total
+        else:
+            out_refs[back - 1][...] = total.astype(jnp.bfloat16)
+
+
+def feature_kernel(student_ref, *refs):
+    total = added(refs[:-1])
     hat, length = unit_rows(student_ref[...])
-    out_ref[...] = (total - hat * jnp.sum(hat * total, axis=1, keepdims=True)) / length
-
-
-def widen_kernel(got_ref, out_ref):
-    out_ref[...] = got_ref[0].astype(jnp.float32)
+    refs[-1][...] = (total - hat * jnp.sum(hat * total, axis=1, keepdims=True)) / length
+
+
+def widen_kernel(place_ref, *refs):
+    *got_refs, out_ref = refs
+    columns = got_refs[0].shape[1]
+    for move, got_ref in enumerate(got_refs):
+        here = pl.ds(pl.multiple_of((place_ref[0] ^ move) * columns, columns), columns)
+        out_ref[:, here] = got_ref[...].astype(jnp.float32)
 
 
 def kernel_body(teacher_feat, student_feat, crop_weight, teacher_v, student_v):
@@ -296,22 +323,44 @@
     kept = teacher_v.shape[1]
     prototypes = kept * fsdp
     count = kept // chips
-    block = lax.axis_index("dp")
-    core = lax.axis_index("fsdp")[None]
+    layers = chips // PLANE
+    chip, core = lax.axis_index("dp"), lax.axis_index("fsdp")
+    place = jnp.stack([chip, core])
     elements = count * crops
     smem, vmem = pl.BlockSpec(memory_space=pltpu.SMEM), pl.BlockSpec(memory_space=pltpu.VMEM)
 
     def swap(values):
         return lax.ppermute(values, "fsdp", [(0, 1), (1, 0)])
 
-    teacher_sent, student_sent = call(
-        units_kernel, (shape((chips, rows, width), bf16), shape((chips, rows, width), bf16))
+    def across(values, move):
+        return lax.ppermute(values, "dp", [(at, at ^ move) for at in range(chips)])
+
+    def along(values, back):
+        return lax.ppermute(values, "dp", [(at, (at + back * PLANE) % chips) for at in range(chips)])
+
+    def gather(values):
+        column = jnp.concatenate([values] + [along(values, back) for back in range(1, layers)])
+        own = [column] + [across(column, move) for move in range(1, PLANE)]
+        return own + [swap(piece) for piece in own]
+
+    def add_up(values):
+        perms = [
+            [(at, at ^ move) for at in range(devices)] for move in range(1, 2 * PLANE)
+        ]
+        total = values
+        for got in [lax.ppermute(values, EVERY, perm) for perm in perms]:
+            total = total + got
+        return [total] + [along(total, back) for back in range(1, layers)]
+
+    teacher_unit, student_unit = call(
+        units_kernel, (shape((rows, width), bf16), shape((rows, width), bf16))
     )(teacher_feat, student_feat)
-    teacher_own = lax.all_to_all(teacher_sent, "dp", 0, 0)
-    teacher_other = swap(teacher_own)
-    student_own = lax.all_to_all(student_sent, "dp", 0, 0)
-    student_other = swap(student_own)
-    weights = jnp.pad(crop_weight[None, :].astype(f32), ((0, 7), (0, LANES - rows)))
+    teacher_got = gather(teacher_unit)
+    student_unit, teacher_got = lax.optimization_barrier((student_unit, teacher_got))
+    student_got = gather(student_unit)
+    weights = lax.dynamic_update_slice(
+        jnp.zeros((crops,), f32), crop_weight.astype(f32), ((2 * chip + core) * rows,)
+    ).reshape(lines, LANES)
 
     tiles = count // TILE
     column = pl.BlockSpec((width, TILE), lambda step, at: (0, at[0] * tiles + step))
@@ -335,7 +384,7 @@
             out_specs=[turned, turned, straight, line],
         ),
     )(
-        block[None],
+        chip[None],
         pltpu.with_memory_space_constraint(teacher_v, pltpu.HBM),
         pltpu.with_memory_space_constraint(student_v, pltpu.HBM),
     )
@@ -343,58 +392,66 @@
     units = pltpu.VMEM((crops, width), bf16)
     total = pltpu.VMEM((8, crops), f32)
     mass, sent = call(
-        functools.partial(teacher_kernel, prototypes),
-        (pltpu.VMEM((count, crops), f32), shape((devices, lines + 8, LANES), bf16)),
+        functools.partial(teacher_kernel, prototypes, layers),
+        (shape((count, crops), f32), shape((2 * lines, LANES), f32)),
         flops=2 * elements * width,
         exps=elements,
-        in_specs=[smem] + [vmem] * 4,
+        in_specs=[smem] + [vmem] * (2 + len(teacher_got)),
         scratch_shapes=[units, total],
-    )(core, teacher_w, teacher_own, teacher_other, weights)
-    got = lax.all_to_all(sent, EVERY, 0, 0)
-    crop_rows = got[:, lines, :rows].astype(f32).reshape(lines, LANES)
+    )(place, teacher_w, *teacher_got, weights)
+    first = got = add_up(sent)
 
     student_mass, student_part, student_turned = call(
-        student_kernel,
-        (pltpu.VMEM((count, crops), f32), shape((lines, LANES), f32), shape((width, crops), bf16)),
+        functools.partial(student_kernel, layers),
+        (shape((count, crops), f32), shape((lines, LANES), f32), shape((width, crops), bf16)),
         flops=2 * elements * width,
         exps=elements,
-        in_specs=[smem] + [vmem] * 3,
+        in_specs=[smem] + [vmem] * (1 + len(student_got)),
         scratch_shapes=[units, total],
-    )(core, student_w, student_own, student_other)
+    )(place, student_w, *student_got)
 
     for sweep in range(1, ITERS):
         extra = sweep == ITERS - 1
         sent, scale = call(
-            functools.partial(sweep_kernel, prototypes, crops, extra),
-            (shape((devices, lines * (1 + extra), LANES), bf16), shape((count, 1), f32)),
+            functools.partial(sweep_kernel, prototypes, crops, layers),
+            (shape((lines * (1 + extra), LANES), f32), shape((count, 1), f32)),
             flops=4 * elements,
             scratch_shapes=[total],
-        )(mass, got, *([student_part] if extra else []))
-        got = lax.all_to_all(sent, EVERY, 0, 0)
+        )(mass, *got, *([student_part] if extra else []))
+        got = add_up(sent)
 
     out_rows = width // chips
-    sent, keep, give = call(
-        gradient_kernel,
-        (
-            shape((chips, out_rows, count), bf16),
-            shape((chips, rows, width), f32),
-            shape((chips, rows, width), bf16),
-        ),
+    *sent, keep, give = call(
+        functools.partial(gradient_kernel, layers, chips),
+        [shape((out_rows, count), bf16)] * chips
+        + [shape((PLANE, layers, rows, width), f32), shape((PLANE, layers, rows, width), bf16)],
         flops=4 * elements * width,
-        in_specs=[smem] + [vmem] * 8,
-        scratch_shapes=[pltpu.VMEM((TILE, crops), bf16), pltpu.VMEM((width, crops), f32)],
-    )(core, mass, student_mass, scale, got, crop_rows, student_turned, student_copy, inverse)
-    grad_got = lax.all_to_all(sent, "dp", 0, 0)
-    paired = call(pair_kernel, shape((chips, rows, width), bf16))(keep, swap(give))
-    feature_got = lax.all_to_all(paired, "dp", 0, 0)
-    grad_feat = call(feature_kernel, shape((rows, width), f32))(feature_got, student_feat)
+        in_specs=[smem] + [vmem] * (6 + 2 * layers),
+        scratch_shapes=[
+            pltpu.VMEM((TILE, crops), bf16),
+            pltpu.VMEM((width, TILE), f32),
+            pltpu.VMEM((width, crops), f32),
+        ],
+    )(place, mass, student_mass, scale, student_turned, student_copy, inverse, *got, *first)
+    other = swap(give)
+    grads = [sent[0]] + [across(sent[move], move) for move in range(1, chips)]
+    own, *pairs = call(
+        pair_kernel,
+        [shape((layers, rows, width), f32)] + [shape((layers, rows, width), bf16)] * (PLANE - 1),
+    )(keep, other)
+    pairs = [own] + [across(pair, move) for move, pair in enumerate(pairs, 1)]
+    own, *planes = call(
+        plane_kernel,
+        [shape((rows, width), f32)] + [shape((rows, width), bf16)] * (layers - 1),
+        in_specs=[smem] + [vmem] * PLANE,
+    )(place, *pairs)
+    planes = [own] + [along(part, layers - back) for back, part in enumerate(planes, 1)]
+    grad_feat = call(feature_kernel, shape((rows, width), f32))(student_feat, *planes)
     grad_v = call(
         widen_kernel,
         shape((out_rows, kept), f32),
-        grid=(chips,),
-        in_specs=[pl.BlockSpec((1, out_rows, count), lambda step: (step, 0, 0))],
-        out_specs=pl.BlockSpec((out_rows, count), lambda step: (0, step)),
-    )(grad_got)
+        in_specs=[smem] + [vmem] * chips,
+    )(place, *grads)
     return (grad_v, grad_feat)
 
 
@@ -404,7 +461,7 @@
     def run(teacher_feat, student_feat, crop_weight, teacher_v, student_v):
         crops = teacher_feat.shape[0]
         count = teacher_v.shape[1] // (dp * fsdp)
-        fits = fsdp == 2 and count % TILE == 0 and crops % 1024 == 0 and 8 * count * crops <= KEPT_BYTES
+        fits = fsdp == 2 and dp in (8, 16) and count % TILE == 0 and crops % 1024 == 0 and 8 * count * crops <= KEPT_BYTES
         every = P(EVERY)
         return jax.shard_map(
             kernel_body if fits else plain_body,

time: 121 us -> 130 us (1.074)
  starting transfers between devices: 16.8 us -> 75.8 us
  blocking collectives: 31.1 us -> 0 us
  local copies, waits for them, and re-layouts: 14.2 us -> 1.45 us
  Pallas kernels: 20.4 us -> 16.7 us
  waiting for transfers between devices: 36.9 us -> 34.1 us
    ppermute x0 -> x63, starting transfers between devices: none -> 73.6 us  [the longest x24 36 us: across(): return lax.ppermute(values, 'dp', [(at, at ^ move) for at in range(chips)])]
    all_to_all x5 -> x0, waiting for transfers between devices: 35.6 us -> none  [the longest x3 19.7 us: kernel_body(): got = lax.all_to_all(sent, EVERY, 0, 0)]
    ppermute x0 -> x63, waiting for transfers between devices: none -> 33.3 us  [the longest x18 19 us: along(): lax.ppermute(values, 'dp', [(at, (at + back * PLANE) % chips) for at in r...]
    all_to_all x2 -> x0, blocking collectives: 31.1 us -> none  [the longest x1 18 us: kernel_body(): teacher_own = lax.all_to_all(teacher_sent, 'dp', 0, 0)]
    all_to_all x5 -> x0, starting transfers between devices: 16.2 us -> none  [the longest x3 9.06 us: kernel_body(): got = lax.all_to_all(sent, EVERY, 0, 0)]
    unnamed x20 -> x12, local copies, waits for them, and re-layouts: 14.2 us -> 1.45 us
    pallas_call x9 -> x10, Pallas kernels: 17.7 us -> 14.1 us  [the longest x1 4.12 us: kernel_body(): call(functools.partial(gradient_kernel, layers, chips), [shape((out_rows,...]
    ppermute x3 -> x9, starting transfers between devices: 0.6 us -> 2.16 us  [swap(): return lax.ppermute(values, 'fsdp', [(0, 1), (1, 0)])]
  transfers between devices with their start and end apart: 8 -> 72, of which waited for: 6 -> 29; matrix products, arithmetic and copies ran while one was open for 0% -> 1% of each run, Pallas kernels for 8% -> 8%
where the time goes in v1:
time: 130 us
  starting transfers between devices  75.8 us (58%)
  waiting for transfers between devices  34.1 us (26%)
  Pallas kernels  16.7 us (13%)
  local copies, waits for them, and re-layouts  1.45 us (1%)
    ppermute x24, starting transfers between devices, across(): return lax.ppermute(values, 'dp', [(at, at ^ move) for at in range(chips)])  36 us
    ppermute x18, starting transfers between devices, along(): lax.ppermute(values, 'dp', [(at, (at + back * PLANE) % chips) for at in r...  20.7 us
    ppermute x18, waiting for transfers between devices, along(): lax.ppermute(values, 'dp', [(at, (at + back * PLANE) % chips) for at in r...  19 us
    ppermute x21, starting transfers between devices, add_up(): lax.ppermute(values, EVERY, perm)  16.9 us
    ppermute x21, waiting for transfers between devices, add_up(): lax.ppermute(values, EVERY, perm)  9.75 us
    ppermute x24, waiting for transfers between devices, across(): return lax.ppermute(values, 'dp', [(at, at ^ move) for at in range(chips)])  4.52 us
    pallas_call x1, Pallas kernels, kernel_body(): call(functools.partial(gradient_kernel, layers, chips), [shape((out_rows,...  4.12 us
    pallas_call x1, Pallas kernels, kernel_body(): call(directions_kernel, (shape((count, width), bf16), shape((count, width...  2.65 us
  transfers between devices with their start and end apart: 72, of which 29 were waited for; matrix products, arithmetic and copies ran while one was open for 1% of the time, Pallas kernels for 8%

profile of v1, /device:TPU:0, one launch (start us, length us, event | category | flops | bytes accessed | tf_op | source)
XLA Modules:
  0.0 129.8 jit_solution(13016823619665247527)
XLA Ops:
  2.2 5.1 %collective-permute-start.2 = (bf16[32,256]{1,0:T(8,128)(2,1)S(1)}, bf16[32,256]{1,0:T(8,128)(2,1)S(1)}, u32[]{:S(2)}, u32[]{:S(2)}) collective-permute-start(bf16[32,256]{1,0:T(8,128)(2,1)S(1)} %get-tuple-element.53), channel_id=1, source_target_pairs={{0,24},{2,26},{4,28},{6,30},{8,0},{10,2},{12,4},{14,6},{16,8},{18,... | collective-permute-start | bytes 49160 | tf_op jit(solution)/shard_map/ppermute | solution.py:339
  7.3 1.0 collective-permute-start
  8.3 4.5 %collective-permute-done = bf16[32,256]{1,0:T(8,128)(2,1)S(1)} collective-permute-done((bf16[32,256]{1,0:T(8,128)(2,1)S(1)}, bf16[32,256]{1,0:T(8,128)(2,1)S(1)}, u32[]{:S(2)}, u32[]{:S(2)}) %collective-permute-start) | collective-permute-done | bytes 16416 | tf_op jit(solution)/shard_map/ppermute | solution.py:339
  12.8 2.5 %collective-permute-start.5 = (bf16[128,256]{1,0:T(8,128)(2,1)S(1)}, bf16[128,256]{1,0:T(8,128)(2,1)S(1)}, u32[]{:S(2)}, u32[]{:S(2)}) collective-permute-start(bf16[128,256]{1,0:T(8,128)(2,1)S(1)} %constant_dynamic-update-slice_fusion.refs_0_), channel_id=1, source_target_pairs={{0,6},{2,4},{4,2},{6,0},{8,14},{10,12},{12,10},{14,8},{16,22},{18,... | collective-permute-start | bytes 196616 | tf_op jit(solution)/shard_map/ppermute | solution.py:336
  17.1 2.6 %shard_map.68 = (bf16[1024,256]{1,0:T(8,128)(2,1)S(1)}, bf16[1024,256]{1,0:T(8,128)(2,1)S(1)}, bf16[256,1024]{1,0:T(8,128)(2,1)S(1)}, f32[1,1024]{1,0:T(1,128)S(1)}) custom-call(s32[1]{0:T(128)} %bitcast.block_ref, bf16[256,16384]{1,0:T(8,128)(2,1)} %teacher_ref.2, bf16[256,16384]{1,0:T(8,128)(2,1)} %student_ref.3), custom_call_target="tpu_custom_call" | custom-call | flops 3145728 | bytes 2621440 | tf_op jit(solution)/shard_map/pallas_call | solution.py:370
  22.9 2.0 %collective-permute-start.10 = (bf16[32,256]{1,0:T(8,128)(2,1)S(1)}, bf16[32,256]{1,0:T(8,128)(2,1)S(1)}, u32[]{:S(2)}, u32[]{:S(2)}) collective-permute-start(bf16[32,256]{1,0:T(8,128)(2,1)S(1)} %get-tuple-element.64), channel_id=1, source_target_pairs={{0,8},{2,10},{4,12},{6,14},{8,16},{10,18},{12,20},{14,22},{16,24},... | collective-permute-start | bytes 49160 | tf_op jit(solution)/shard_map/ppermute | solution.py:339
  25.0 2.4 %shard_map.70 = (f32[1024,1024]{1,0:T(8,128)S(1)}, f32[16,128]{1,0:T(8,128)S(1)}) custom-call(s32[2]{0:T(128)S(1)} %pad_add_fusion.place_ref, bf16[1024,256]{1,0:T(8,128)(2,1)S(1)} %get-tuple-element.51.directions_ref, bf16[128,256]{1,0:T(8,128)(2,1)S(1)} %constant_dynamic-update-slice_fusion.refs_0_, bf16[128,256]{1,0:T(8,128)(2,1)S(1)} %collective-permute-done.3.refs_1_, ...), custom_call_target="tpu_custom_call" | custom-call | flops 536870912 | tf_op jit(solution)/shard_map/pallas_call | solution.py:394
  27.4 1.6 %collective-permute-start.26 = (f32[16,128]{1,0:T(8,128)S(1)}, f32[16,128]{1,0:T(8,128)S(1)}, u32[]{:S(2)}, u32[]{:S(2)}) collective-permute-start(f32[16,128]{1,0:T(8,128)S(1)} %get-tuple-element.66), channel_id=1, source_target_pairs={{0,7},{1,6},{2,5},{3,4},{4,3},{5,2},{6,1},{7,0},{8,15},{9,14},{10,... | collective-permute-start | bytes 24584 | tf_op jit(solution)/shard_map/ppermute | solution.py:351
  29.0 1.0 collective-permute-start.25
  29.9 1.4 %collective-permute-start.24 = (f32[16,128]{1,0:T(8,128)S(1)}, f32[16,128]{1,0:T(8,128)S(1)}, u32[]{:S(2)}, u32[]{:S(2)}) collective-permute-start(f32[16,128]{1,0:T(8,128)S(1)} %get-tuple-element.66), channel_id=1, source_target_pairs={{0,5},{1,4},{2,7},{3,6},{4,1},{5,0},{6,3},{7,2},{8,13},{9,12},{10,... | collective-permute-start | bytes 24584 | tf_op jit(solution)/shard_map/ppermute | solution.py:351
  31.8 0.8 collective-permute-start.22
  32.6 1.0 collective-permute-done.25
  34.2 2.0 %collective-permute-start.15 = (bf16[128,256]{1,0:T(8,128)(2,1)S(1)}, bf16[128,256]{1,0:T(8,128)(2,1)S(1)}, u32[]{:S(2)}, u32[]{:S(2)}) collective-permute-start(bf16[128,256]{1,0:T(8,128)(2,1)S(1)} %constant_dynamic-update-slice_fusion.4.refs_0_), channel_id=1, source_target_pairs={{0,6},{2,4},{4,2},{6,0},{8,14},{10,12},{12,10},{14,8},{16,22},{18,... | collective-permute-start | bytes 196616 | tf_op jit(solution)/shard_map/ppermute | solution.py:336
  36.2 1.0 collective-permute-start.14
  37.7 2.1 %collective-permute-start.29 = (f32[16,128]{1,0:T(8,128)S(1)}, f32[16,128]{1,0:T(8,128)S(1)}, u32[]{:S(2)}, u32[]{:S(2)}) collective-permute-start(f32[16,128]{1,0:T(8,128)S(1)} %add_add_fusion.1.refs_0_.refs_4_), channel_id=1, source_target_pairs={{0,24},{2,26},{4,28},{6,30},{8,0},{10,2},{12,4},{14,6},{16,8},{18,... | collective-permute-start | bytes 24584 | tf_op jit(solution)/shard_map/ppermute | solution.py:339
  40.2 1.3 collective-permute-done.29.refs_3_.refs_7_
  41.4 0.9 collective-permute-start.27
  42.3 2.1 %collective-permute-done.28.refs_2_.refs_6_ = f32[16,128]{1,0:T(8,128)S(1)} collective-permute-done((f32[16,128]{1,0:T(8,128)S(1)}, f32[16,128]{1,0:T(8,128)S(1)}, u32[]{:S(2)}, u32[]{:S(2)}) %collective-permute-start.28) | collective-permute-done | bytes 8224 | tf_op jit(solution)/shard_map/ppermute | solution.py:339
  44.4 2.5 %collective-permute-done.27.refs_1_.refs_5_ = f32[16,128]{1,0:T(8,128)S(1)} collective-permute-done((f32[16,128]{1,0:T(8,128)S(1)}, f32[16,128]{1,0:T(8,128)S(1)}, u32[]{:S(2)}, u32[]{:S(2)}) %collective-permute-start.27) | collective-permute-done | bytes 8224 | tf_op jit(solution)/shard_map/ppermute | solution.py:339
  46.9 1.5 %shard_map.72 = (f32[8,128]{1,0:T(8,128)S(1)}, f32[1024,1]{1,0:T(8,128)}) custom-call(f32[1024,1024]{1,0:T(8,128)S(1)} %get-tuple-element.62.mass_ref.teacher_ref, f32[16,128]{1,0:T(8,128)S(1)} %add_add_fusion.1.refs_0_.refs_4_, f32[16,128]{1,0:T(8,128)S(1)} %collective-permute-done.27.refs_1_.refs_5_, ...), custom_call_target="tpu_custom_call" | custom-call | flops 4194304 | tf_op jit(solution)/shard_map/pallas_call | solution.py:415
  48.5 1.9 %collective-permute-start.35 = (f32[8,128]{1,0:T(8,128)S(1)}, f32[8,128]{1,0:T(8,128)S(1)}, u32[]{:S(2)}, u32[]{:S(2)}) collective-permute-start(f32[8,128]{1,0:T(8,128)S(1)} %get-tuple-element.67), channel_id=1, source_target_pairs={{0,6},{1,7},{2,4},{3,5},{4,2},{5,3},{6,0},{7,1},{8,14},{9,15},{10,... | collective-permute-start | bytes 12296 | tf_op jit(solution)/shard_map/ppermute | solution.py:351
  50.4 2.0 %collective-permute-done.36 = f32[8,128]{1,0:T(8,128)S(1)} collective-permute-done((f32[8,128]{1,0:T(8,128)S(1)}, f32[8,128]{1,0:T(8,128)S(1)}, u32[]{:S(2)}, u32[]{:S(2)}) %collective-permute-start.36) | collective-permute-done | bytes 4128 | tf_op jit(solution)/shard_map/ppermute | solution.py:351
  53.0 1.0 collective-permute-start.33
  53.9 1.5 %collective-permute-done.34 = f32[8,128]{1,0:T(8,128)S(1)} collective-permute-done((f32[8,128]{1,0:T(8,128)S(1)}, f32[8,128]{1,0:T(8,128)S(1)}, u32[]{:S(2)}, u32[]{:S(2)}) %collective-permute-start.34) | collective-permute-done | bytes 4128 | tf_op jit(solution)/shard_map/ppermute | solution.py:351
  55.8 0.8 collective-permute-done.33
  56.6 1.4 %collective-permute-start.31 = (f32[8,128]{1,0:T(8,128)S(1)}, f32[8,128]{1,0:T(8,128)S(1)}, u32[]{:S(2)}, u32[]{:S(2)}) collective-permute-start(f32[8,128]{1,0:T(8,128)S(1)} %get-tuple-element.67), channel_id=1, source_target_pairs={{0,2},{1,3},{2,0},{3,1},{4,6},{5,7},{6,4},{7,5},{8,10},{9,11},{10,... | collective-permute-start | bytes 12296 | tf_op jit(solution)/shard_map/ppermute | solution.py:351
  58.6 1.6 %collective-permute-done.31 = f32[8,128]{1,0:T(8,128)S(1)} collective-permute-done((f32[8,128]{1,0:T(8,128)S(1)}, f32[8,128]{1,0:T(8,128)S(1)}, u32[]{:S(2)}, u32[]{:S(2)}) %collective-permute-start.31) | collective-permute-done | bytes 4128 | tf_op jit(solution)/shard_map/ppermute | solution.py:351
  61.3 2.1 %collective-permute-start.39 = (f32[8,128]{1,0:T(8,128)S(1)}, f32[8,128]{1,0:T(8,128)S(1)}, u32[]{:S(2)}, u32[]{:S(2)}) collective-permute-start(f32[8,128]{1,0:T(8,128)S(1)} %add_add_fusion.2.refs_0_), channel_id=1, source_target_pairs={{0,24},{2,26},{4,28},{6,30},{8,0},{10,2},{12,4},{14,6},{16,8},{18,... | collective-permute-start | bytes 12296 | tf_op jit(solution)/shard_map/ppermute | solution.py:339
  64.1 2.2 %shard_map.71 = (f32[1024,1024]{1,0:T(8,128)S(1)}, f32[8,128]{1,0:T(8,128)S(1)}, bf16[256,1024]{1,0:T(8,128)(2,1)S(1)}) custom-call(s32[2]{0:T(128)S(1)} %pad_add_fusion.place_ref, bf16[1024,256]{1,0:T(8,128)(2,1)S(1)} %get-tuple-element.63.directions_ref, bf16[128,256]{1,0:T(8,128)(2,1)S(1)} %constant_dynamic-update-slice_fusion.4.refs_0_, ...), custom_call_target="tpu_custom_call" | custom-call | flops 536870912 | tf_op jit(solution)/shard_map/pallas_call | solution.py:404
  66.3 1.6 %collective-permute-done.38.refs_2_ = f32[8,128]{1,0:T(8,128)S(1)} collective-permute-done((f32[8,128]{1,0:T(8,128)S(1)}, f32[8,128]{1,0:T(8,128)S(1)}, u32[]{:S(2)}, u32[]{:S(2)}) %collective-permute-start.38) | collective-permute-done | bytes 4128 | tf_op jit(solution)/shard_map/ppermute | solution.py:339
  67.9 1.0 collective-permute-done.37.refs_1_
  68.8 0.7 shard_map.73
  69.6 1.7 %collective-permute-start.45 = (f32[16,128]{1,0:T(8,128)S(1)}, f32[16,128]{1,0:T(8,128)S(1)}, u32[]{:S(2)}, u32[]{:S(2)}) collective-permute-start(f32[16,128]{1,0:T(8,128)S(1)} %get-tuple-element.73), channel_id=1, source_target_pairs={{0,6},{1,7},{2,4},{3,5},{4,2},{5,3},{6,0},{7,1},{8,14},{9,15},{10,... | collective-permute-start | bytes 24584 | tf_op jit(solution)/shard_map/ppermute | solution.py:351
  71.4 1.4 %collective-permute-start.44 = (f32[16,128]{1,0:T(8,128)S(1)}, f32[16,128]{1,0:T(8,128)S(1)}, u32[]{:S(2)}, u32[]{:S(2)}) collective-permute-start(f32[16,128]{1,0:T(8,128)S(1)} %get-tuple-element.73), channel_id=1, source_target_pairs={{0,5},{1,4},{2,7},{3,6},{4,1},{5,0},{6,3},{7,2},{8,13},{9,12},{10,... | collective-permute-start | bytes 24584 | tf_op jit(solution)/shard_map/ppermute | solution.py:351
  72.7 1.3 %collective-permute-start.43 = (f32[16,128]{1,0:T(8,128)S(1)}, f32[16,128]{1,0:T(8,128)S(1)}, u32[]{:S(2)}, u32[]{:S(2)}) collective-permute-start(f32[16,128]{1,0:T(8,128)S(1)} %get-tuple-element.73), channel_id=1, source_target_pairs={{0,4},{1,5},{2,6},{3,7},{4,0},{5,1},{6,2},{7,3},{8,12},{9,13},{10,... | collective-permute-start | bytes 24584 | tf_op jit(solution)/shard_map/ppermute | solution.py:351
  74.0 1.5 %collective-permute-start.41 = (f32[16,128]{1,0:T(8,128)S(1)}, f32[16,128]{1,0:T(8,128)S(1)}, u32[]{:S(2)}, u32[]{:S(2)}) collective-permute-start(f32[16,128]{1,0:T(8,128)S(1)} %get-tuple-element.73), channel_id=1, source_target_pairs={{0,2},{1,3},{2,0},{3,1},{4,6},{5,7},{6,4},{7,5},{8,10},{9,11},{10,... | collective-permute-start | bytes 24584 | tf_op jit(solution)/shard_map/ppermute | solution.py:351
  76.4 0.8 collective-permute-done.42
  77.7 1.3 %collective-permute-start.49 = (f32[16,128]{1,0:T(8,128)S(1)}, f32[16,128]{1,0:T(8,128)S(1)}, u32[]{:S(2)}, u32[]{:S(2)}) collective-permute-start(f32[16,128]{1,0:T(8,128)S(1)} %add_add_fusion.refs_0_), channel_id=1, source_target_pairs={{0,24},{2,26},{4,28},{6,30},{8,0},{10,2},{12,4},{14,6},{16,8},{18,... | collective-permute-start | bytes 24584 | tf_op jit(solution)/shard_map/ppermute | solution.py:339
  79.8 1.1 collective-permute-start.47
  81.4 2.1 %collective-permute-done.48.refs_2_ = f32[16,128]{1,0:T(8,128)S(1)} collective-permute-done((f32[16,128]{1,0:T(8,128)S(1)}, f32[16,128]{1,0:T(8,128)S(1)}, u32[]{:S(2)}, u32[]{:S(2)}) %collective-permute-start.48) | collective-permute-done | bytes 8224 | tf_op jit(solution)/shard_map/ppermute | solution.py:339
  83.6 1.6 %collective-permute-done.47.refs_1_ = f32[16,128]{1,0:T(8,128)S(1)} collective-permute-done((f32[16,128]{1,0:T(8,128)S(1)}, f32[16,128]{1,0:T(8,128)S(1)}, u32[]{:S(2)}, u32[]{:S(2)}) %collective-permute-start.47) | collective-permute-done | bytes 8224 | tf_op jit(solution)/shard_map/ppermute | solution.py:339
  85.2 4.1 %shard_map.74 = (bf16[16,1024]{1,0:T(8,128)(2,1)S(1)}, bf16[16,1024]{1,0:T(8,128)(2,1)S(1)}, bf16[16,1024]{1,0:T(8,128)(2,1)S(1)}, bf16[16,1024]{1,0:T(8,128)(2,...) custom-call(s32[2]{0:T(128)S(1)} %pad_add_fusion.place_ref, ...), custom_call_target="tpu_custom_call" | custom-call | flops 1073741824 | tf_op jit(solution)/shard_map/pallas_call | solution.py:424
  89.4 1.3 collective-permute-start.50
  90.7 0.8 collective-permute-start.51
  91.5 1.5 %collective-permute-start.52 = (bf16[16,1024]{1,0:T(8,128)(2,1)S(1)}, bf16[16,1024]{1,0:T(8,128)(2,1)S(1)}, u32[]{:S(2)}, u32[]{:S(2)}) collective-permute-start(bf16[16,1024]{1,0:T(8,128)(2,1)S(1)} %get-tuple-element.77), channel_id=1, source_target_pairs={{0,6},{2,4},{4,2},{6,0},{8,14},{10,12},{12,10},{14,8},{16,22},{18,... | collective-permute-start | bytes 98312 | tf_op jit(solution)/shard_map/ppermute | solution.py:336
  93.4 2.2 %collective-permute-start.54 = (bf16[16,1024]{1,0:T(8,128)(2,1)S(1)}, bf16[16,1024]{1,0:T(8,128)(2,1)S(1)}, u32[]{:S(2)}, u32[]{:S(2)}) collective-permute-start(bf16[16,1024]{1,0:T(8,128)(2,1)S(1)} %get-tuple-element.79), channel_id=1, source_target_pairs={{0,10},{2,8},{4,14},{6,12},{8,2},{10,0},{12,6},{14,4},{16,26},{18,... | collective-permute-start | bytes 98312 | tf_op jit(solution)/shard_map/ppermute | solution.py:336
  96.3 2.5 %collective-permute-start.56 = (bf16[16,1024]{1,0:T(8,128)(2,1)S(1)}, bf16[16,1024]{1,0:T(8,128)(2,1)S(1)}, u32[]{:S(2)}, u32[]{:S(2)}) collective-permute-start(bf16[16,1024]{1,0:T(8,128)(2,1)S(1)} %get-tuple-element.81), channel_id=1, source_target_pairs={{0,14},{2,12},{4,10},{6,8},{8,6},{10,4},{12,2},{14,0},{16,30},{18,... | collective-permute-start | bytes 98312 | tf_op jit(solution)/shard_map/ppermute | solution.py:336
  99.3 0.9 collective-permute-start.66
  100.2 0.8 collective-permute-start.67
  101.1 1.8 %collective-permute-start.68 = (bf16[4,32,256]{2,1,0:T(8,128)(2,1)S(1)}, bf16[4,32,256]{2,1,0:T(8,128)(2,1)S(1)}, u32[]{:S(2)}, u32[]{:S(2)}) collective-permute-start(bf16[4,32,256]{2,1,0:T(8,128)(2,1)S(1)} %get-tuple-element.95), channel_id=1, source_target_pairs={{0,6},{2,4},{4,2},{6,0},{8,14},{10,12},{12,10},{14,8},{16,22},{18,... | collective-permute-start | bytes 196616 | tf_op jit(solution)/shard_map/ppermute | solution.py:336
  102.9 3.2 %collective-permute-start.58 = (bf16[16,1024]{1,0:T(8,128)(2,1)S(1)}, bf16[16,1024]{1,0:T(8,128)(2,1)S(1)}, u32[]{:S(2)}, u32[]{:S(2)}) collective-permute-start(bf16[16,1024]{1,0:T(8,128)(2,1)S(1)} %get-tuple-element.83), channel_id=1, source_target_pairs={{0,18},{2,16},{4,22},{6,20},{8,26},{10,24},{12,30},{14,28},{16,2},... | collective-permute-start | bytes 98312 | tf_op jit(solution)/shard_map/ppermute | solution.py:336
  106.4 2.6 %collective-permute-done.58.refs_9_ = bf16[16,1024]{1,0:T(8,128)(2,1)S(1)} collective-permute-done((bf16[16,1024]{1,0:T(8,128)(2,1)S(1)}, bf16[16,1024]{1,0:T(8,128)(2,1)S(1)}, u32[]{:S(2)}, u32[]{:S(2)}) %collective-permute-start.58) | collective-permute-done | bytes 32800 | tf_op jit(solution)/shard_map/ppermute | solution.py:336
  108.9 3.0 %collective-permute-start.60 = (bf16[16,1024]{1,0:T(8,128)(2,1)S(1)}, bf16[16,1024]{1,0:T(8,128)(2,1)S(1)}, u32[]{:S(2)}, u32[]{:S(2)}) collective-permute-start(bf16[16,1024]{1,0:T(8,128)(2,1)S(1)} %get-tuple-element.85), channel_id=1, source_target_pairs={{0,22},{2,20},{4,18},{6,16},{8,30},{10,28},{12,26},{14,24},{16,6},... | collective-permute-start | bytes 98312 | tf_op jit(solution)/shard_map/ppermute | solution.py:336
  112.4 0.9 collective-permute-start.61
  113.3 3.1 %collective-permute-start.62 = (bf16[16,1024]{1,0:T(8,128)(2,1)S(1)}, bf16[16,1024]{1,0:T(8,128)(2,1)S(1)}, u32[]{:S(2)}, u32[]{:S(2)}) collective-permute-start(bf16[16,1024]{1,0:T(8,128)(2,1)S(1)} %get-tuple-element.87), channel_id=1, source_target_pairs={{0,26},{2,24},{4,30},{6,28},{8,18},{10,16},{12,22},{14,20},{16,10}... | collective-permute-start | bytes 98312 | tf_op jit(solution)/shard_map/ppermute | solution.py:336
  116.4 1.8 %collective-permute-start.63 = (bf16[16,1024]{1,0:T(8,128)(2,1)S(1)}, bf16[16,1024]{1,0:T(8,128)(2,1)S(1)}, u32[]{:S(2)}, u32[]{:S(2)}) collective-permute-start(bf16[16,1024]{1,0:T(8,128)(2,1)S(1)} %get-tuple-element.88), channel_id=1, source_target_pairs={{0,28},{2,30},{4,24},{6,26},{8,20},{10,22},{12,16},{14,18},{16,12}... | collective-permute-start | bytes 98312 | tf_op jit(solution)/shard_map/ppermute | solution.py:336
  118.2 3.7 %collective-permute-start.64 = (bf16[16,1024]{1,0:T(8,128)(2,1)S(1)}, bf16[16,1024]{1,0:T(8,128)(2,1)S(1)}, u32[]{:S(2)}, u32[]{:S(2)}) collective-permute-start(bf16[16,1024]{1,0:T(8,128)(2,1)S(1)} %get-tuple-element.89), channel_id=1, source_target_pairs={{0,30},{2,28},{4,26},{6,24},{8,22},{10,20},{12,18},{14,16},{16,14}... | collective-permute-start | bytes 98312 | tf_op jit(solution)/shard_map/ppermute | solution.py:336
  122.5 0.9 collective-permute-start.69
  123.4 1.2 collective-permute-start.71
  124.6 1.0 collective-permute-done.64.refs_15_
  125.7 1.6 %shard_map.75 = f32[16,16384]{1,0:T(8,128)} custom-call(s32[2]{0:T(128)S(1)} %pad_add_fusion.place_ref, bf16[16,1024]{1,0:T(8,128)(2,1)S(1)} %get-tuple-element.74.refs_0_, bf16[16,1024]{1,0:T(8,128)(2,1)S(1)} %collective-permute-done.50.refs_1_, bf16[16,1024]{1,0:T(8,128)(2,1)S(1)} %collective-permute-done.51.refs_2_, ...), custom_call_target="tpu_custom_call" | custom-call | tf_op jit(solution)/shard_map/pallas_call | solution.py:450
  127.3 0.8 collective-permute-done.70.refs_2_
  128.1 1.0 collective-permute-done.71.refs_3_
  129.0 0.8 shard_map.78
  (111 shorter events, 17.5 us)
Async XLA Ops:
  2.2 10.7 %collective-permute-start.2 = (bf16[32,256]{1,0:T(8,128)(2,1)S(1)}, bf16[32,256]{1,0:T(8,128)(2,1)S(1)}, u32[]{:S(2)}, u32[]{:S(2)}) collective-permute-start(bf16[32,256]{1,0:T(8,128)(2,1)S(1)} %get-tuple-element.53), channel_id=1, source_target_pairs={{0,24},{2,26},{4,28},{6,30},{8,0},{10,2},{12,4},{14,6},{16,8},{18,... | collective-permute-start | bytes 49160 | tf_op jit(solution)/shard_map/ppermute | solution.py:339
  7.3 5.5 %collective-permute-start.1 = (bf16[32,256]{1,0:T(8,128)(2,1)S(1)}, bf16[32,256]{1,0:T(8,128)(2,1)S(1)}, u32[]{:S(2)}, u32[]{:S(2)}) collective-permute-start(bf16[32,256]{1,0:T(8,128)(2,1)S(1)} %get-tuple-element.53), channel_id=1, source_target_pairs={{0,16},{2,18},{4,20},{6,22},{8,24},{10,26},{12,28},{14,30},{16,0},... | collective-permute-start | bytes 49160 | tf_op jit(solution)/shard_map/ppermute | solution.py:339
  7.3 5.5 %collective-permute-start = (bf16[32,256]{1,0:T(8,128)(2,1)S(1)}, bf16[32,256]{1,0:T(8,128)(2,1)S(1)}, u32[]{:S(2)}, u32[]{:S(2)}) collective-permute-start(bf16[32,256]{1,0:T(8,128)(2,1)S(1)} %get-tuple-element.53), channel_id=1, source_target_pairs={{0,8},{2,10},{4,12},{6,14},{8,16},{10,18},{12,20},{14,22},{16,24},... | collective-permute-start | bytes 49160 | tf_op jit(solution)/shard_map/ppermute | solution.py:339
  12.8 7.0 %collective-permute-start.5 = (bf16[128,256]{1,0:T(8,128)(2,1)S(1)}, bf16[128,256]{1,0:T(8,128)(2,1)S(1)}, u32[]{:S(2)}, u32[]{:S(2)}) collective-permute-start(bf16[128,256]{1,0:T(8,128)(2,1)S(1)} %constant_dynamic-update-slice_fusion.refs_0_), channel_id=1, source_target_pairs={{0,6},{2,4},{4,2},{6,0},{8,14},{10,12},{12,10},{14,8},{16,22},{18,... | collective-permute-start | bytes 196616 | tf_op jit(solution)/shard_map/ppermute | solution.py:336
  15.4 5.0 %collective-permute-start.4 = (bf16[128,256]{1,0:T(8,128)(2,1)S(1)}, bf16[128,256]{1,0:T(8,128)(2,1)S(1)}, u32[]{:S(2)}, u32[]{:S(2)}) collective-permute-start(bf16[128,256]{1,0:T(8,128)(2,1)S(1)} %constant_dynamic-update-slice_fusion.refs_0_), channel_id=1, source_target_pairs={{0,4},{2,6},{4,0},{6,2},{8,12},{10,14},{12,8},{14,10},{16,20},{18,... | collective-permute-start | bytes 196616 | tf_op jit(solution)/shard_map/ppermute | solution.py:336
  15.9 4.6 %collective-permute-start.3 = (bf16[128,256]{1,0:T(8,128)(2,1)S(1)}, bf16[128,256]{1,0:T(8,128)(2,1)S(1)}, u32[]{:S(2)}, u32[]{:S(2)}) collective-permute-start(bf16[128,256]{1,0:T(8,128)(2,1)S(1)} %constant_dynamic-update-slice_fusion.refs_0_), channel_id=1, source_target_pairs={{0,2},{2,0},{4,6},{6,4},{8,10},{10,8},{12,14},{14,12},{16,18},{18,... | collective-permute-start | bytes 196616 | tf_op jit(solution)/shard_map/ppermute | solution.py:336
  21.8 12.3 %collective-permute-start.12 = (bf16[32,256]{1,0:T(8,128)(2,1)S(1)}, bf16[32,256]{1,0:T(8,128)(2,1)S(1)}, u32[]{:S(2)}, u32[]{:S(2)}) collective-permute-start(bf16[32,256]{1,0:T(8,128)(2,1)S(1)} %get-tuple-element.64), channel_id=1, source_target_pairs={{0,24},{2,26},{4,28},{6,30},{8,0},{10,2},{12,4},{14,6},{16,8},{18,... | collective-permute-start | bytes 49160 | tf_op jit(solution)/shard_map/ppermute | solution.py:339
  22.4 8.9 %collective-permute-start.11 = (bf16[32,256]{1,0:T(8,128)(2,1)S(1)}, bf16[32,256]{1,0:T(8,128)(2,1)S(1)}, u32[]{:S(2)}, u32[]{:S(2)}) collective-permute-start(bf16[32,256]{1,0:T(8,128)(2,1)S(1)} %get-tuple-element.64), channel_id=1, source_target_pairs={{0,16},{2,18},{4,20},{6,22},{8,24},{10,26},{12,28},{14,30},{16,0},... | collective-permute-start | bytes 49160 | tf_op jit(solution)/shard_map/ppermute | solution.py:339
  22.9 7.0 %collective-permute-start.10 = (bf16[32,256]{1,0:T(8,128)(2,1)S(1)}, bf16[32,256]{1,0:T(8,128)(2,1)S(1)}, u32[]{:S(2)}, u32[]{:S(2)}) collective-permute-start(bf16[32,256]{1,0:T(8,128)(2,1)S(1)} %get-tuple-element.64), channel_id=1, source_target_pairs={{0,8},{2,10},{4,12},{6,14},{8,16},{10,18},{12,20},{14,22},{16,24},... | collective-permute-start | bytes 49160 | tf_op jit(solution)/shard_map/ppermute | solution.py:339
  27.4 4.5 %collective-permute-start.26 = (f32[16,128]{1,0:T(8,128)S(1)}, f32[16,128]{1,0:T(8,128)S(1)}, u32[]{:S(2)}, u32[]{:S(2)}) collective-permute-start(f32[16,128]{1,0:T(8,128)S(1)} %get-tuple-element.66), channel_id=1, source_target_pairs={{0,7},{1,6},{2,5},{3,4},{4,3},{5,2},{6,1},{7,0},{8,15},{9,14},{10,... | collective-permute-start | bytes 24584 | tf_op jit(solution)/shard_map/ppermute | solution.py:351
  29.0 4.6 %collective-permute-start.25 = (f32[16,128]{1,0:T(8,128)S(1)}, f32[16,128]{1,0:T(8,128)S(1)}, u32[]{:S(2)}, u32[]{:S(2)}) collective-permute-start(f32[16,128]{1,0:T(8,128)S(1)} %get-tuple-element.66), channel_id=1, source_target_pairs={{0,6},{1,7},{2,4},{3,5},{4,2},{5,3},{6,0},{7,1},{8,14},{9,15},{10,... | collective-permute-start | bytes 24584 | tf_op jit(solution)/shard_map/ppermute | solution.py:351
  29.9 4.2 %collective-permute-start.24 = (f32[16,128]{1,0:T(8,128)S(1)}, f32[16,128]{1,0:T(8,128)S(1)}, u32[]{:S(2)}, u32[]{:S(2)}) collective-permute-start(f32[16,128]{1,0:T(8,128)S(1)} %get-tuple-element.66), channel_id=1, source_target_pairs={{0,5},{1,4},{2,7},{3,6},{4,1},{5,0},{6,3},{7,2},{8,13},{9,12},{10,... | collective-permute-start | bytes 24584 | tf_op jit(solution)/shard_map/ppermute | solution.py:351
  31.3 4.8 %collective-permute-start.23 = (f32[16,128]{1,0:T(8,128)S(1)}, f32[16,128]{1,0:T(8,128)S(1)}, u32[]{:S(2)}, u32[]{:S(2)}) collective-permute-start(f32[16,128]{1,0:T(8,128)S(1)} %get-tuple-element.66), channel_id=1, source_target_pairs={{0,4},{1,5},{2,6},{3,7},{4,0},{5,1},{6,2},{7,3},{8,12},{9,13},{10,... | collective-permute-start | bytes 24584 | tf_op jit(solution)/shard_map/ppermute | solution.py:351
  31.8 5.4 %collective-permute-start.22 = (f32[16,128]{1,0:T(8,128)S(1)}, f32[16,128]{1,0:T(8,128)S(1)}, u32[]{:S(2)}, u32[]{:S(2)}) collective-permute-start(f32[16,128]{1,0:T(8,128)S(1)} %get-tuple-element.66), channel_id=1, source_target_pairs={{0,3},{1,2},{2,1},{3,0},{4,7},{5,6},{6,5},{7,4},{8,11},{9,10},{10,... | collective-permute-start | bytes 24584 | tf_op jit(solution)/shard_map/ppermute | solution.py:351
  33.6 4.1 %collective-permute-start.21 = (f32[16,128]{1,0:T(8,128)S(1)}, f32[16,128]{1,0:T(8,128)S(1)}, u32[]{:S(2)}, u32[]{:S(2)}) collective-permute-start(f32[16,128]{1,0:T(8,128)S(1)} %get-tuple-element.66), channel_id=1, source_target_pairs={{0,2},{1,3},{2,0},{3,1},{4,6},{5,7},{6,4},{7,5},{8,10},{9,11},{10,... | collective-permute-start | bytes 24584 | tf_op jit(solution)/shard_map/ppermute | solution.py:351
  34.1 3.6 %collective-permute-start.20 = (f32[16,128]{1,0:T(8,128)S(1)}, f32[16,128]{1,0:T(8,128)S(1)}, u32[]{:S(2)}, u32[]{:S(2)}) collective-permute-start(f32[16,128]{1,0:T(8,128)S(1)} %get-tuple-element.66), channel_id=1, source_target_pairs={{0,1},{1,0},{2,3},{3,2},{4,5},{5,4},{6,7},{7,6},{8,9},{9,8},{10,11... | collective-permute-start | bytes 24584 | tf_op jit(solution)/shard_map/ppermute | solution.py:351
  34.2 26.1 %collective-permute-start.15 = (bf16[128,256]{1,0:T(8,128)(2,1)S(1)}, bf16[128,256]{1,0:T(8,128)(2,1)S(1)}, u32[]{:S(2)}, u32[]{:S(2)}) collective-permute-start(bf16[128,256]{1,0:T(8,128)(2,1)S(1)} %constant_dynamic-update-slice_fusion.4.refs_0_), channel_id=1, source_target_pairs={{0,6},{2,4},{4,2},{6,0},{8,14},{10,12},{12,10},{14,8},{16,22},{18,... | collective-permute-start | bytes 196616 | tf_op jit(solution)/shard_map/ppermute | solution.py:336
  36.2 24.6 %collective-permute-start.14 = (bf16[128,256]{1,0:T(8,128)(2,1)S(1)}, bf16[128,256]{1,0:T(8,128)(2,1)S(1)}, u32[]{:S(2)}, u32[]{:S(2)}) collective-permute-start(bf16[128,256]{1,0:T(8,128)(2,1)S(1)} %constant_dynamic-update-slice_fusion.4.refs_0_), channel_id=1, source_target_pairs={{0,4},{2,6},{4,0},{6,2},{8,12},{10,14},{12,8},{14,10},{16,20},{18,... | collective-permute-start | bytes 196616 | tf_op jit(solution)/shard_map/ppermute | solution.py:336
  37.2 23.6 %collective-permute-start.13 = (bf16[128,256]{1,0:T(8,128)(2,1)S(1)}, bf16[128,256]{1,0:T(8,128)(2,1)S(1)}, u32[]{:S(2)}, u32[]{:S(2)}) collective-permute-start(bf16[128,256]{1,0:T(8,128)(2,1)S(1)} %constant_dynamic-update-slice_fusion.4.refs_0_), channel_id=1, source_target_pairs={{0,2},{2,0},{4,6},{6,4},{8,10},{10,8},{12,14},{14,12},{16,18},{18,... | collective-permute-start | bytes 196616 | tf_op jit(solution)/shard_map/ppermute | solution.py:336
  37.7 3.7 %collective-permute-start.29 = (f32[16,128]{1,0:T(8,128)S(1)}, f32[16,128]{1,0:T(8,128)S(1)}, u32[]{:S(2)}, u32[]{:S(2)}) collective-permute-start(f32[16,128]{1,0:T(8,128)S(1)} %add_add_fusion.1.refs_0_.refs_4_), channel_id=1, source_target_pairs={{0,24},{2,26},{4,28},{6,30},{8,0},{10,2},{12,4},{14,6},{16,8},{18,... | collective-permute-start | bytes 24584 | tf_op jit(solution)/shard_map/ppermute | solution.py:339
  39.9 4.5 %collective-permute-start.28 = (f32[16,128]{1,0:T(8,128)S(1)}, f32[16,128]{1,0:T(8,128)S(1)}, u32[]{:S(2)}, u32[]{:S(2)}) collective-permute-start(f32[16,128]{1,0:T(8,128)S(1)} %add_add_fusion.1.refs_0_.refs_4_), channel_id=1, source_target_pairs={{0,16},{2,18},{4,20},{6,22},{8,24},{10,26},{12,28},{14,30},{16,0},... | collective-permute-start | bytes 24584 | tf_op jit(solution)/shard_map/ppermute | solution.py:339
  41.4 5.5 %collective-permute-start.27 = (f32[16,128]{1,0:T(8,128)S(1)}, f32[16,128]{1,0:T(8,128)S(1)}, u32[]{:S(2)}, u32[]{:S(2)}) collective-permute-start(f32[16,128]{1,0:T(8,128)S(1)} %add_add_fusion.1.refs_0_.refs_4_), channel_id=1, source_target_pairs={{0,8},{2,10},{4,12},{6,14},{8,16},{10,18},{12,20},{14,22},{16,24},... | collective-permute-start | bytes 24584 | tf_op jit(solution)/shard_map/ppermute | solution.py:339
  48.4 3.9 %collective-permute-start.36 = (f32[8,128]{1,0:T(8,128)S(1)}, f32[8,128]{1,0:T(8,128)S(1)}, u32[]{:S(2)}, u32[]{:S(2)}) collective-permute-start(f32[8,128]{1,0:T(8,128)S(1)} %get-tuple-element.67), channel_id=1, source_target_pairs={{0,7},{1,6},{2,5},{3,4},{4,3},{5,2},{6,1},{7,0},{8,15},{9,14},{10,... | collective-permute-start | bytes 12296 | tf_op jit(solution)/shard_map/ppermute | solution.py:351
  48.5 4.5 %collective-permute-start.35 = (f32[8,128]{1,0:T(8,128)S(1)}, f32[8,128]{1,0:T(8,128)S(1)}, u32[]{:S(2)}, u32[]{:S(2)}) collective-permute-start(f32[8,128]{1,0:T(8,128)S(1)} %get-tuple-element.67), channel_id=1, source_target_pairs={{0,6},{1,7},{2,4},{3,5},{4,2},{5,3},{6,0},{7,1},{8,14},{9,15},{10,... | collective-permute-start | bytes 12296 | tf_op jit(solution)/shard_map/ppermute | solution.py:351
  53.0 3.6 %collective-permute-start.33 = (f32[8,128]{1,0:T(8,128)S(1)}, f32[8,128]{1,0:T(8,128)S(1)}, u32[]{:S(2)}, u32[]{:S(2)}) collective-permute-start(f32[8,128]{1,0:T(8,128)S(1)} %get-tuple-element.67), channel_id=1, source_target_pairs={{0,4},{1,5},{2,6},{3,7},{4,0},{5,1},{6,2},{7,3},{8,12},{9,13},{10,... | collective-permute-start | bytes 12296 | tf_op jit(solution)/shard_map/ppermute | solution.py:351
  56.6 3.6 %collective-permute-start.31 = (f32[8,128]{1,0:T(8,128)S(1)}, f32[8,128]{1,0:T(8,128)S(1)}, u32[]{:S(2)}, u32[]{:S(2)}) collective-permute-start(f32[8,128]{1,0:T(8,128)S(1)} %get-tuple-element.67), channel_id=1, source_target_pairs={{0,2},{1,3},{2,0},{3,1},{4,6},{5,7},{6,4},{7,5},{8,10},{9,11},{10,... | collective-permute-start | bytes 12296 | tf_op jit(solution)/shard_map/ppermute | solution.py:351
  60.2 3.1 %collective-permute-start.16 = (bf16[128,256]{1,0:T(8,128)(2,1)S(1)}, bf16[128,256]{1,0:T(8,128)(2,1)S(1)}, u32[]{:S(2)}, u32[]{:S(2)}) collective-permute-start(bf16[128,256]{1,0:T(8,128)(2,1)S(1)} %constant_dynamic-update-slice_fusion.4.refs_0_), channel_id=1, source_target_pairs={{0,1},{1,0},{2,3},{3,2},{4,5},{5,4},{6,7},{7,6},{8,9},{9,8},{10,11... | collective-permute-start | bytes 196616 | tf_op jit(solution)/shard_map/ppermute | solution.py:333
  60.2 3.1 %collective-permute-start.19 = (bf16[128,256]{1,0:T(8,128)(2,1)S(1)}, bf16[128,256]{1,0:T(8,128)(2,1)S(1)}, u32[]{:S(2)}, u32[]{:S(2)}) collective-permute-start(bf16[128,256]{1,0:T(8,128)(2,1)S(1)} %collective-permute-done.15.refs_3_), channel_id=1, source_target_pairs={{0,1},{1,0},{2,3},{3,2},{4,5},{5,4},{6,7},{7,6},{8,9},{9,8},{10,11... | collective-permute-start | bytes 196616 | tf_op jit(solution)/shard_map/ppermute | solution.py:333
  60.7 3.3 %collective-permute-start.18 = (bf16[128,256]{1,0:T(8,128)(2,1)S(1)}, bf16[128,256]{1,0:T(8,128)(2,1)S(1)}, u32[]{:S(2)}, u32[]{:S(2)}) collective-permute-start(bf16[128,256]{1,0:T(8,128)(2,1)S(1)} %collective-permute-done.14.refs_2_), channel_id=1, source_target_pairs={{0,1},{1,0},{2,3},{3,2},{4,5},{5,4},{6,7},{7,6},{8,9},{9,8},{10,11... | collective-permute-start | bytes 196616 | tf_op jit(solution)/shard_map/ppermute | solution.py:333
  60.8 3.3 %collective-permute-start.17 = (bf16[128,256]{1,0:T(8,128)(2,1)S(1)}, bf16[128,256]{1,0:T(8,128)(2,1)S(1)}, u32[]{:S(2)}, u32[]{:S(2)}) collective-permute-start(bf16[128,256]{1,0:T(8,128)(2,1)S(1)} %collective-permute-done.13.refs_1_), channel_id=1, source_target_pairs={{0,1},{1,0},{2,3},{3,2},{4,5},{5,4},{6,7},{7,6},{8,9},{9,8},{10,11... | collective-permute-start | bytes 196616 | tf_op jit(solution)/shard_map/ppermute | solution.py:333
  61.3 5.0 %collective-permute-start.39 = (f32[8,128]{1,0:T(8,128)S(1)}, f32[8,128]{1,0:T(8,128)S(1)}, u32[]{:S(2)}, u32[]{:S(2)}) collective-permute-start(f32[8,128]{1,0:T(8,128)S(1)} %add_add_fusion.2.refs_0_), channel_id=1, source_target_pairs={{0,24},{2,26},{4,28},{6,30},{8,0},{10,2},{12,4},{14,6},{16,8},{18,... | collective-permute-start | bytes 12296 | tf_op jit(solution)/shard_map/ppermute | solution.py:339
  63.3 4.5 %collective-permute-start.38 = (f32[8,128]{1,0:T(8,128)S(1)}, f32[8,128]{1,0:T(8,128)S(1)}, u32[]{:S(2)}, u32[]{:S(2)}) collective-permute-start(f32[8,128]{1,0:T(8,128)S(1)} %add_add_fusion.2.refs_0_), channel_id=1, source_target_pairs={{0,16},{2,18},{4,20},{6,22},{8,24},{10,26},{12,28},{14,30},{16,0},... | collective-permute-start | bytes 12296 | tf_op jit(solution)/shard_map/ppermute | solution.py:339
  63.4 5.5 %collective-permute-start.37 = (f32[8,128]{1,0:T(8,128)S(1)}, f32[8,128]{1,0:T(8,128)S(1)}, u32[]{:S(2)}, u32[]{:S(2)}) collective-permute-start(f32[8,128]{1,0:T(8,128)S(1)} %add_add_fusion.2.refs_0_), channel_id=1, source_target_pairs={{0,8},{2,10},{4,12},{6,14},{8,16},{10,18},{12,20},{14,22},{16,24},... | collective-permute-start | bytes 12296 | tf_op jit(solution)/shard_map/ppermute | solution.py:339
  69.6 4.5 %collective-permute-start.46 = (f32[16,128]{1,0:T(8,128)S(1)}, f32[16,128]{1,0:T(8,128)S(1)}, u32[]{:S(2)}, u32[]{:S(2)}) collective-permute-start(f32[16,128]{1,0:T(8,128)S(1)} %get-tuple-element.73), channel_id=1, source_target_pairs={{0,7},{1,6},{2,5},{3,4},{4,3},{5,2},{6,1},{7,0},{8,15},{9,14},{10,... | collective-permute-start | bytes 24584 | tf_op jit(solution)/shard_map/ppermute | solution.py:351
  69.6 5.8 %collective-permute-start.45 = (f32[16,128]{1,0:T(8,128)S(1)}, f32[16,128]{1,0:T(8,128)S(1)}, u32[]{:S(2)}, u32[]{:S(2)}) collective-permute-start(f32[16,128]{1,0:T(8,128)S(1)} %get-tuple-element.73), channel_id=1, source_target_pairs={{0,6},{1,7},{2,4},{3,5},{4,2},{5,3},{6,0},{7,1},{8,14},{9,15},{10,... | collective-permute-start | bytes 24584 | tf_op jit(solution)/shard_map/ppermute | solution.py:351
  71.4 4.5 %collective-permute-start.44 = (f32[16,128]{1,0:T(8,128)S(1)}, f32[16,128]{1,0:T(8,128)S(1)}, u32[]{:S(2)}, u32[]{:S(2)}) collective-permute-start(f32[16,128]{1,0:T(8,128)S(1)} %get-tuple-element.73), channel_id=1, source_target_pairs={{0,5},{1,4},{2,7},{3,6},{4,1},{5,0},{6,3},{7,2},{8,13},{9,12},{10,... | collective-permute-start | bytes 24584 | tf_op jit(solution)/shard_map/ppermute | solution.py:351
  72.7 3.7 %collective-permute-start.43 = (f32[16,128]{1,0:T(8,128)S(1)}, f32[16,128]{1,0:T(8,128)S(1)}, u32[]{:S(2)}, u32[]{:S(2)}) collective-permute-start(f32[16,128]{1,0:T(8,128)S(1)} %get-tuple-element.73), channel_id=1, source_target_pairs={{0,4},{1,5},{2,6},{3,7},{4,0},{5,1},{6,2},{7,3},{8,12},{9,13},{10,... | collective-permute-start | bytes 24584 | tf_op jit(solution)/shard_map/ppermute | solution.py:351
  74.0 3.1 %collective-permute-start.42 = (f32[16,128]{1,0:T(8,128)S(1)}, f32[16,128]{1,0:T(8,128)S(1)}, u32[]{:S(2)}, u32[]{:S(2)}) collective-permute-start(f32[16,128]{1,0:T(8,128)S(1)} %get-tuple-element.73), channel_id=1, source_target_pairs={{0,3},{1,2},{2,1},{3,0},{4,7},{5,6},{6,5},{7,4},{8,11},{9,10},{10,... | collective-permute-start | bytes 24584 | tf_op jit(solution)/shard_map/ppermute | solution.py:351
  74.0 3.7 %collective-permute-start.41 = (f32[16,128]{1,0:T(8,128)S(1)}, f32[16,128]{1,0:T(8,128)S(1)}, u32[]{:S(2)}, u32[]{:S(2)}) collective-permute-start(f32[16,128]{1,0:T(8,128)S(1)} %get-tuple-element.73), channel_id=1, source_target_pairs={{0,2},{1,3},{2,0},{3,1},{4,6},{5,7},{6,4},{7,5},{8,10},{9,11},{10,... | collective-permute-start | bytes 24584 | tf_op jit(solution)/shard_map/ppermute | solution.py:351
  77.7 3.7 %collective-permute-start.49 = (f32[16,128]{1,0:T(8,128)S(1)}, f32[16,128]{1,0:T(8,128)S(1)}, u32[]{:S(2)}, u32[]{:S(2)}) collective-permute-start(f32[16,128]{1,0:T(8,128)S(1)} %add_add_fusion.refs_0_), channel_id=1, source_target_pairs={{0,24},{2,26},{4,28},{6,30},{8,0},{10,2},{12,4},{14,6},{16,8},{18,... | collective-permute-start | bytes 24584 | tf_op jit(solution)/shard_map/ppermute | solution.py:339
  79.0 4.5 %collective-permute-start.48 = (f32[16,128]{1,0:T(8,128)S(1)}, f32[16,128]{1,0:T(8,128)S(1)}, u32[]{:S(2)}, u32[]{:S(2)}) collective-permute-start(f32[16,128]{1,0:T(8,128)S(1)} %add_add_fusion.refs_0_), channel_id=1, source_target_pairs={{0,16},{2,18},{4,20},{6,22},{8,24},{10,26},{12,28},{14,30},{16,0},... | collective-permute-start | bytes 24584 | tf_op jit(solution)/shard_map/ppermute | solution.py:339
  79.8 5.4 %collective-permute-start.47 = (f32[16,128]{1,0:T(8,128)S(1)}, f32[16,128]{1,0:T(8,128)S(1)}, u32[]{:S(2)}, u32[]{:S(2)}) collective-permute-start(f32[16,128]{1,0:T(8,128)S(1)} %add_add_fusion.refs_0_), channel_id=1, source_target_pairs={{0,8},{2,10},{4,12},{6,14},{8,16},{10,18},{12,20},{14,22},{16,24},... | collective-permute-start | bytes 24584 | tf_op jit(solution)/shard_map/ppermute | solution.py:339
  89.3 9.5 %collective-permute-start.65 = (bf16[4,4,32,256]{3,2,1,0:T(8,128)(2,1)S(1)}, bf16[4,4,32,256]{3,2,1,0:T(8,128)(2,1)S(1)}, u32[]{:S(2)}, u32[]{:S(2)}) collective-permute-start(bf16[4,4,32,256]{3,2,1,0:T(8,128)(2,1)S(1)} %get-tuple-element.91), channel_id=1, source_target_pairs={{0,1},{1,0},{2,3},{3,2},{4,5},{5,4},{6,7},{7,6},{8,9},{9,8},{10,11... | collective-permute-start | bytes 786440 | tf_op jit(solution)/shard_map/ppermute | solution.py:333
  89.4 4.0 %collective-permute-start.50 = (bf16[16,1024]{1,0:T(8,128)(2,1)S(1)}, bf16[16,1024]{1,0:T(8,128)(2,1)S(1)}, u32[]{:S(2)}, u32[]{:S(2)}) collective-permute-start(bf16[16,1024]{1,0:T(8,128)(2,1)S(1)} %get-tuple-element.75), channel_id=1, source_target_pairs={{0,2},{2,0},{4,6},{6,4},{8,10},{10,8},{12,14},{14,12},{16,18},{18,... | collective-permute-start | bytes 98312 | tf_op jit(solution)/shard_map/ppermute | solution.py:336
  90.7 5.0 %collective-permute-start.51 = (bf16[16,1024]{1,0:T(8,128)(2,1)S(1)}, bf16[16,1024]{1,0:T(8,128)(2,1)S(1)}, u32[]{:S(2)}, u32[]{:S(2)}) collective-permute-start(bf16[16,1024]{1,0:T(8,128)(2,1)S(1)} %get-tuple-element.76), channel_id=1, source_target_pairs={{0,4},{2,6},{4,0},{6,2},{8,12},{10,14},{12,8},{14,10},{16,20},{18,... | collective-permute-start | bytes 98312 | tf_op jit(solution)/shard_map/ppermute | solution.py:336
  91.5 4.8 %collective-permute-start.52 = (bf16[16,1024]{1,0:T(8,128)(2,1)S(1)}, bf16[16,1024]{1,0:T(8,128)(2,1)S(1)}, u32[]{:S(2)}, u32[]{:S(2)}) collective-permute-start(bf16[16,1024]{1,0:T(8,128)(2,1)S(1)} %get-tuple-element.77), channel_id=1, source_target_pairs={{0,6},{2,4},{4,2},{6,0},{8,14},{10,12},{12,10},{14,8},{16,22},{18,... | collective-permute-start | bytes 98312 | tf_op jit(solution)/shard_map/ppermute | solution.py:336
  93.0 6.3 %collective-permute-start.53 = (bf16[16,1024]{1,0:T(8,128)(2,1)S(1)}, bf16[16,1024]{1,0:T(8,128)(2,1)S(1)}, u32[]{:S(2)}, u32[]{:S(2)}) collective-permute-start(bf16[16,1024]{1,0:T(8,128)(2,1)S(1)} %get-tuple-element.78), channel_id=1, source_target_pairs={{0,8},{2,10},{4,12},{6,14},{8,0},{10,2},{12,4},{14,6},{16,24},{18,... | collective-permute-start | bytes 98312 | tf_op jit(solution)/shard_map/ppermute | solution.py:336
  93.4 6.8 %collective-permute-start.54 = (bf16[16,1024]{1,0:T(8,128)(2,1)S(1)}, bf16[16,1024]{1,0:T(8,128)(2,1)S(1)}, u32[]{:S(2)}, u32[]{:S(2)}) collective-permute-start(bf16[16,1024]{1,0:T(8,128)(2,1)S(1)} %get-tuple-element.79), channel_id=1, source_target_pairs={{0,10},{2,8},{4,14},{6,12},{8,2},{10,0},{12,6},{14,4},{16,26},{18,... | collective-permute-start | bytes 98312 | tf_op jit(solution)/shard_map/ppermute | solution.py:336
  95.6 5.5 %collective-permute-start.55 = (bf16[16,1024]{1,0:T(8,128)(2,1)S(1)}, bf16[16,1024]{1,0:T(8,128)(2,1)S(1)}, u32[]{:S(2)}, u32[]{:S(2)}) collective-permute-start(bf16[16,1024]{1,0:T(8,128)(2,1)S(1)} %get-tuple-element.80), channel_id=1, source_target_pairs={{0,12},{2,14},{4,8},{6,10},{8,4},{10,6},{12,0},{14,2},{16,28},{18,... | collective-permute-start | bytes 98312 | tf_op jit(solution)/shard_map/ppermute | solution.py:336
  96.3 6.6 %collective-permute-start.56 = (bf16[16,1024]{1,0:T(8,128)(2,1)S(1)}, bf16[16,1024]{1,0:T(8,128)(2,1)S(1)}, u32[]{:S(2)}, u32[]{:S(2)}) collective-permute-start(bf16[16,1024]{1,0:T(8,128)(2,1)S(1)} %get-tuple-element.81), channel_id=1, source_target_pairs={{0,14},{2,12},{4,10},{6,8},{8,6},{10,4},{12,2},{14,0},{16,30},{18,... | collective-permute-start | bytes 98312 | tf_op jit(solution)/shard_map/ppermute | solution.py:336
  98.8 7.2 %collective-permute-start.57 = (bf16[16,1024]{1,0:T(8,128)(2,1)S(1)}, bf16[16,1024]{1,0:T(8,128)(2,1)S(1)}, u32[]{:S(2)}, u32[]{:S(2)}) collective-permute-start(bf16[16,1024]{1,0:T(8,128)(2,1)S(1)} %get-tuple-element.82), channel_id=1, source_target_pairs={{0,16},{2,18},{4,20},{6,22},{8,24},{10,26},{12,28},{14,30},{16,0},... | collective-permute-start | bytes 98312 | tf_op jit(solution)/shard_map/ppermute | solution.py:336
  99.3 14.0 %collective-permute-start.66 = (bf16[4,32,256]{2,1,0:T(8,128)(2,1)S(1)}, bf16[4,32,256]{2,1,0:T(8,128)(2,1)S(1)}, u32[]{:S(2)}, u32[]{:S(2)}) collective-permute-start(bf16[4,32,256]{2,1,0:T(8,128)(2,1)S(1)} %get-tuple-element.93), channel_id=1, source_target_pairs={{0,2},{2,0},{4,6},{6,4},{8,10},{10,8},{12,14},{14,12},{16,18},{18,... | collective-permute-start | bytes 196616 | tf_op jit(solution)/shard_map/ppermute | solution.py:336
  100.2 16.2 %collective-permute-start.67 = (bf16[4,32,256]{2,1,0:T(8,128)(2,1)S(1)}, bf16[4,32,256]{2,1,0:T(8,128)(2,1)S(1)}, u32[]{:S(2)}, u32[]{:S(2)}) collective-permute-start(bf16[4,32,256]{2,1,0:T(8,128)(2,1)S(1)} %get-tuple-element.94), channel_id=1, source_target_pairs={{0,4},{2,6},{4,0},{6,2},{8,12},{10,14},{12,8},{14,10},{16,20},{18,... | collective-permute-start | bytes 196616 | tf_op jit(solution)/shard_map/ppermute | solution.py:336
  101.1 17.1 %collective-permute-start.68 = (bf16[4,32,256]{2,1,0:T(8,128)(2,1)S(1)}, bf16[4,32,256]{2,1,0:T(8,128)(2,1)S(1)}, u32[]{:S(2)}, u32[]{:S(2)}) collective-permute-start(bf16[4,32,256]{2,1,0:T(8,128)(2,1)S(1)} %get-tuple-element.95), channel_id=1, source_target_pairs={{0,6},{2,4},{4,2},{6,0},{8,14},{10,12},{12,10},{14,8},{16,22},{18,... | collective-permute-start | bytes 196616 | tf_op jit(solution)/shard_map/ppermute | solution.py:336
  102.9 6.1 %collective-permute-start.58 = (bf16[16,1024]{1,0:T(8,128)(2,1)S(1)}, bf16[16,1024]{1,0:T(8,128)(2,1)S(1)}, u32[]{:S(2)}, u32[]{:S(2)}) collective-permute-start(bf16[16,1024]{1,0:T(8,128)(2,1)S(1)} %get-tuple-element.83), channel_id=1, source_target_pairs={{0,18},{2,16},{4,22},{6,20},{8,26},{10,24},{12,30},{14,28},{16,2},... | collective-permute-start | bytes 98312 | tf_op jit(solution)/shard_map/ppermute | solution.py:336
  106.0 6.4 %collective-permute-start.59 = (bf16[16,1024]{1,0:T(8,128)(2,1)S(1)}, bf16[16,1024]{1,0:T(8,128)(2,1)S(1)}, u32[]{:S(2)}, u32[]{:S(2)}) collective-permute-start(bf16[16,1024]{1,0:T(8,128)(2,1)S(1)} %get-tuple-element.84), channel_id=1, source_target_pairs={{0,20},{2,22},{4,16},{6,18},{8,28},{10,30},{12,24},{14,26},{16,4},... | collective-permute-start | bytes 98312 | tf_op jit(solution)/shard_map/ppermute | solution.py:336
  108.9 13.5 %collective-permute-start.60 = (bf16[16,1024]{1,0:T(8,128)(2,1)S(1)}, bf16[16,1024]{1,0:T(8,128)(2,1)S(1)}, u32[]{:S(2)}, u32[]{:S(2)}) collective-permute-start(bf16[16,1024]{1,0:T(8,128)(2,1)S(1)} %get-tuple-element.85), channel_id=1, source_target_pairs={{0,22},{2,20},{4,18},{6,16},{8,30},{10,28},{12,26},{14,24},{16,6},... | collective-permute-start | bytes 98312 | tf_op jit(solution)/shard_map/ppermute | solution.py:336
  112.4 11.0 %collective-permute-start.61 = (bf16[16,1024]{1,0:T(8,128)(2,1)S(1)}, bf16[16,1024]{1,0:T(8,128)(2,1)S(1)}, u32[]{:S(2)}, u32[]{:S(2)}) collective-permute-start(bf16[16,1024]{1,0:T(8,128)(2,1)S(1)} %get-tuple-element.86), channel_id=1, source_target_pairs={{0,24},{2,26},{4,28},{6,30},{8,16},{10,18},{12,20},{14,22},{16,8},... | collective-permute-start | bytes 98312 | tf_op jit(solution)/shard_map/ppermute | solution.py:336
  113.3 10.1 %collective-permute-start.62 = (bf16[16,1024]{1,0:T(8,128)(2,1)S(1)}, bf16[16,1024]{1,0:T(8,128)(2,1)S(1)}, u32[]{:S(2)}, u32[]{:S(2)}) collective-permute-start(bf16[16,1024]{1,0:T(8,128)(2,1)S(1)} %get-tuple-element.87), channel_id=1, source_target_pairs={{0,26},{2,24},{4,30},{6,28},{8,18},{10,16},{12,22},{14,20},{16,10}... | collective-permute-start | bytes 98312 | tf_op jit(solution)/shard_map/ppermute | solution.py:336
  116.4 8.2 %collective-permute-start.63 = (bf16[16,1024]{1,0:T(8,128)(2,1)S(1)}, bf16[16,1024]{1,0:T(8,128)(2,1)S(1)}, u32[]{:S(2)}, u32[]{:S(2)}) collective-permute-start(bf16[16,1024]{1,0:T(8,128)(2,1)S(1)} %get-tuple-element.88), channel_id=1, source_target_pairs={{0,28},{2,30},{4,24},{6,26},{8,20},{10,22},{12,16},{14,18},{16,12}... | collective-permute-start | bytes 98312 | tf_op jit(solution)/shard_map/ppermute | solution.py:336
  118.2 7.5 %collective-permute-start.64 = (bf16[16,1024]{1,0:T(8,128)(2,1)S(1)}, bf16[16,1024]{1,0:T(8,128)(2,1)S(1)}, u32[]{:S(2)}, u32[]{:S(2)}) collective-permute-start(bf16[16,1024]{1,0:T(8,128)(2,1)S(1)} %get-tuple-element.89), channel_id=1, source_target_pairs={{0,30},{2,28},{4,26},{6,24},{8,22},{10,20},{12,18},{14,16},{16,14}... | collective-permute-start | bytes 98312 | tf_op jit(solution)/shard_map/ppermute | solution.py:336
  122.5 4.8 %collective-permute-start.69 = (bf16[32,256]{1,0:T(8,128)(2,1)S(1)}, bf16[32,256]{1,0:T(8,128)(2,1)S(1)}, u32[]{:S(2)}, u32[]{:S(2)}) collective-permute-start(bf16[32,256]{1,0:T(8,128)(2,1)S(1)} %get-tuple-element.97), channel_id=1, source_target_pairs={{0,24},{2,26},{4,28},{6,30},{8,0},{10,2},{12,4},{14,6},{16,8},{18,... | collective-permute-start | bytes 49160 | tf_op jit(solution)/shard_map/ppermute | solution.py:339
  123.4 4.6 %collective-permute-start.70 = (bf16[32,256]{1,0:T(8,128)(2,1)S(1)}, bf16[32,256]{1,0:T(8,128)(2,1)S(1)}, u32[]{:S(2)}, u32[]{:S(2)}) collective-permute-start(bf16[32,256]{1,0:T(8,128)(2,1)S(1)} %get-tuple-element.98), channel_id=1, source_target_pairs={{0,16},{2,18},{4,20},{6,22},{8,24},{10,26},{12,28},{14,30},{16,0},... | collective-permute-start | bytes 49160 | tf_op jit(solution)/shard_map/ppermute | solution.py:339
  123.4 5.6 %collective-permute-start.71 = (bf16[32,256]{1,0:T(8,128)(2,1)S(1)}, bf16[32,256]{1,0:T(8,128)(2,1)S(1)}, u32[]{:S(2)}, u32[]{:S(2)}) collective-permute-start(bf16[32,256]{1,0:T(8,128)(2,1)S(1)} %get-tuple-element.99), channel_id=1, source_target_pairs={{0,8},{2,10},{4,12},{6,14},{8,16},{10,18},{12,20},{14,22},{16,24},... | collective-permute-start | bytes 49160 | tf_op jit(solution)/shard_map/ppermute | solution.py:339
  (11 other events, 78.0 us)
